TPU v7x, 256 devices: a whole 4x4x8 slice. The times are simulated.
256 devices in a mesh: depth: 32 (over z, y), height: 8 (over x, core).
Axes of the slice: x: 4, y: 4, z: 8, core: 2. Of those that a mesh axis runs over, the one named last changes fastest.
Arguments:
- features: bfloat16 [32, 384, 256, 128], P(None, 'depth', 'height'), may hold values from -6 to 6
- head_weight: bfloat16 [3, 32], replicated, may hold values from -1 to 1
- head_bias: float32 [3], replicated, may hold values from -3 to 3
- labels: int32 [3, 384, 256, 128], P(None, 'depth', 'height'), may hold values from 0 to 1
- label_skeleton: int32 [3, 384, 256, 128], P(None, 'depth', 'height'), may hold values from 0 to 1
Outputs:
- loss: float32 [], replicated
- grad_features: bfloat16 [32, 384, 256, 128], P(None, 'depth', 'height')
- head_update: float32 [3, 32], replicated
- bias_update: float32 [3], replicated
All inputs are finite; a program needn't handle non-finite values.
Results may differ from a plain program's by a relative error of at most 0.0016.
Values sent between devices are 32-bit elements; how exact they have to be, the bound alone decides.
No kernel may reach another device: no remote copies, remote signals or barrier semaphores. Data moves between devices by JAX's collectives and lax.ppermute only.
A program may use at most 128 MiB of HBM per device.

v0:
```python
import jax
import jax.numpy as jnp
from jax import lax
from jax.experimental import pallas as pl
from jax.experimental.pallas import tpu as pltpu
from jax.sharding import PartitionSpec as P

ITERS = 3
TAU = 0.1
SHARP = 0.05
ALPHA = 0.3
BETA = 0.7
HALO = 10
LHALO = 5
ROWS = 80
OFF = 24
NB = 4


def class_term(totals):
    tp, sp, sl, sky, sk, lsp, ls = [totals[i] for i in range(7)]
    prec = (sky + 1.0) / (sk + 1.0)
    sens = (lsp + 1.0) / (ls + 1.0)
    cldice = 1.0 - 2.0 * prec * sens / (prec + sens)
    tversky = (tp + 1.0) / (tp + ALPHA * (sp - tp) + BETA * (sl - tp) + 1.0)
    return cldice + 1.0 - tversky


def shift(value, axis, step):
    n = lax.axis_size(axis)
    pairs = [(i, i + step) for i in range(n) if 0 <= i + step < n]
    return lax.ppermute(value, axis, pairs)


def exchange(value, dim, width, axis):
    n = value.shape[dim]
    before = shift(lax.slice_in_dim(value, n - width, n, axis=dim), axis, 1)
    after = shift(lax.slice_in_dim(value, 0, width, axis=dim), axis, -1)
    return before, after


def wide_sum(s, lane):
    width = s.shape[-1]
    left = jnp.where(lane == 0, 0.0, pltpu.roll(s, 1, 1))
    right = jnp.where(lane == width - 1, 0.0, pltpu.roll(s, width - 1, 1))
    return s + left + right


def boxes(load, d, r0, nr, lane):
    h = []
    for i in range(NB + 2):
        h.append(load(d + i - 1, r0 - 1, nr) + load(d + i - 1, r0, nr) + load(d + i - 1, r0 + 1, nr))
    out = []
    for i in range(0, NB, 2):
        mid = h[i + 1] + h[i + 2]
        out.append(wide_sum(h[i] + mid, lane))
        out.append(wide_sum(mid + h[i + 3], lane))
    return out


def sweep(first, last, body):
    count = -(-(last - first) // NB)

    def step(i, carry):
        body(jnp.minimum(first + i * NB, last - NB))
        return carry

    lax.fori_loop(0, count, step, 0)


def core(
    e_own, e_dlo, e_dhi, e_hlo, e_hhi, l_own, l_dlo, l_dhi, l_hlo, l_hhi, p_own, k_own,
    ga_ref, gb_ref, part_ref,
    E, R, X, U, V, Q, L,
):
    depth, height = p_own.shape[1], p_own.shape[2]
    planes = depth + 2 * HALO
    wd = p_own.shape[3]
    lane8 = lax.broadcasted_iota(jnp.int32, (8, wd), 1)
    base = HALO - LHALO
    E[0, :, OFF - HALO - 8 : OFF, :] = jnp.zeros((planes, HALO + 8, wd), jnp.float32)
    E[0, :, OFF + height : OFF + height + HALO + 8, :] = jnp.zeros((planes, HALO + 8, wd), jnp.float32)
    E[0, HALO : HALO + depth, OFF : OFF + height, :] = e_own[0]
    E[0, 0:HALO, OFF : OFF + height, :] = e_dlo[0]
    E[0, HALO + depth :, OFF : OFF + height, :] = e_dhi[0]
    E[0, :, OFF - HALO : OFF, :] = e_hlo[0]
    E[0, :, OFF + height : OFF + height + HALO, :] = e_hhi[0]
    lplanes = depth + 2 * LHALO
    L[:, OFF - 8 : OFF, :] = jnp.zeros((lplanes, 8, wd), jnp.float32)
    L[:, OFF + height : OFF + height + 8, :] = jnp.zeros((lplanes, 8, wd), jnp.float32)
    L[LHALO : LHALO + depth, OFF : OFF + height, :] = l_own[0]
    L[0:LHALO, OFF : OFF + height, :] = l_dlo[0]
    L[LHALO + depth :, OFF : OFF + height, :] = l_dhi[0]
    L[:, OFF - LHALO : OFF, :] = l_hlo[0]
    L[:, OFF + height : OFF + height + LHALO, :] = l_hhi[0]

    w0, wn = OFF - 8, height + 16
    lane = lax.broadcasted_iota(jnp.int32, (wn, wd), 1)
    lane_big = lax.broadcasted_iota(jnp.int32, (wn + 16, wd), 1)

    for j in range(ITERS + 1):
        r0, nr, ln = (w0 - 8, wn + 16, lane_big) if j == 0 else (w0, wn, lane)

        def erode(d, j=j, r0=r0, nr=nr, ln=ln):
            outs = boxes(lambda a, b, n: E[j, a, pl.ds(b, n), :], d, r0, nr, ln)
            for i, s in enumerate(outs):
                live = E[0, d + i, pl.ds(r0, nr), :] > 0.0
                E[j + 1, d + i, pl.ds(r0, nr), :] = jnp.where(live, s, 0.0)
                R[j, d + i, pl.ds(r0, nr), :] = jnp.where(live, 1.0 / s, 0.0)

        sweep(j + 1, planes - j - 1, erode)

    for j in range(ITERS + 1):

        def dilate(d, j=j):
            outs = boxes(lambda a, b, n: R[j, a, pl.ds(b, n), :], d, w0, wn, lane)
            for i, s in enumerate(outs):
                live = E[0, d + i, pl.ds(w0, wn), :] > 0.0
                rd = 1.0 / s
                t = rd / E[j, d + i, pl.ds(w0, wn), :]
                U[j, d + i - base, pl.ds(w0, wn), :] = jnp.where(live, rd, 0.0)
                X[j, d + i - base, pl.ds(w0, wn), :] = jnp.where(live, t * t, 0.0)

        sweep(base, planes - base, dilate)

    def point(i, carry):
        d = i // (wn // 8)
        r = pl.multiple_of(w0 + 8 * (i % (wn // 8)), 8)
        x = [X[j, d, pl.ds(r, 8), :] for j in range(ITERS + 1)]
        opx = [1.0 + v for v in x]
        delta = [SHARP * jnp.log(v) for v in opx]
        skel = delta[0]
        om, su = [None], [None]
        for j in range(1, ITERS + 1):
            om.append(1.0 - skel)
            e = jnp.exp(delta[j] * om[j] * (1.0 / SHARP))
            ope = 1.0 + e
            skel = skel + SHARP * jnp.log(ope)
            su.append(e / ope)
        lab = L[d, pl.ds(r, 8), :]
        g = None
        for j in range(ITERS, 0, -1):
            sj = su[j] if g is None else su[j] * g
            gv = sj * om[j] * (x[j] / opx[j])
            keep = 1.0 - su[j] * delta[j]
            g = keep if g is None else g * keep
            u = gv * U[j, d, pl.ds(r, 8), :]
            X[j, d, pl.ds(r, 8), :] = gv
            U[j, d, pl.ds(r, 8), :] = u
            V[j, d, pl.ds(r, 8), :] = u * lab
        gv = g * (x[0] / opx[0])
        u = gv * U[0, d, pl.ds(r, 8), :]
        X[0, d, pl.ds(r, 8), :] = gv
        U[0, d, pl.ds(r, 8), :] = u
        V[0, d, pl.ds(r, 8), :] = u * lab
        own = (d >= LHALO) & (d < LHALO + depth) & (r >= OFF) & (r < OFF + height)
        f = jnp.where(own, 1.0, 0.0)
        skel = skel * f
        return carry[0] + skel * lab, carry[1] + skel

    zero = jnp.zeros((8, wd), jnp.float32)
    sky, sk = lax.fori_loop(0, lplanes * (wn // 8), point, (zero, zero))
    part_ref[0, 3] = sky
    part_ref[0, 4] = sk

    for j in range(ITERS + 1, 0, -1):
        now, nxt = j % 2, (j + 1) % 2

        def back(d, j=j, now=now, nxt=nxt):
            b = d - base
            for side, src in ((0, V), (1, U)):
                du = boxes(lambda a, c, n: src[j - 1, a, pl.ds(c, n), :], b, w0, wn, lane)
                if j <= ITERS:
                    dq = boxes(lambda a, c, n: Q[side, nxt, a, pl.ds(c, n), :], b, w0, wn, lane)
                for i in range(NB):
                    live = E[0, d + i, pl.ds(w0, wn), :] > 0.0
                    r = R[j - 1, d + i, pl.ds(w0, wn), :]
                    v = -r * du[i]
                    if j <= ITERS:
                        gv = X[j, b + i, pl.ds(w0, wn), :]
                        if side == 0:
                            gv = gv * L[b + i, pl.ds(w0, wn), :]
                        v = r * (gv + v) + dq[i]
                        v = jnp.where(live, v, 0.0)
                    else:
                        v = r * v
                    Q[side, now, b + i, pl.ds(w0, wn), :] = v

        first = HALO - j
        sweep(first, planes - first, back)

    lane_own = lax.broadcasted_iota(jnp.int32, (height, wd), 1)

    def last(d):
        b = d - base
        o = d - HALO
        for side, out in ((0, ga_ref), (1, gb_ref)):
            dq = boxes(lambda a, c, n: Q[side, 1, a, pl.ds(c, n), :], b, OFF, height, lane_own)
            for i in range(NB):
                gv = X[0, b + i, pl.ds(OFF, height), :]
                if side == 0:
                    gv = gv * L[b + i, pl.ds(OFF, height), :]
                out[0, o + i] = gv + E[0, d + i, pl.ds(OFF, height), :] * dq[i]

    sweep(HALO, HALO + depth, last)

    def sums(o, carry):
        tp, sp, sl, lsp, ls = carry
        for t in range(height // 8):
            p = p_own[0, o, pl.ds(8 * t, 8), :]
            y = l_own[0, o, pl.ds(8 * t, 8), :]
            k = k_own[0, o, pl.ds(8 * t, 8), :].astype(jnp.float32)
            tp, sp, sl, lsp, ls = tp + p * y, sp + p, sl + y, lsp + k * p, ls + k
        return tp, sp, sl, lsp, ls

    tp, sp, sl, lsp, ls = lax.fori_loop(0, depth, sums, (zero,) * 5)
    part_ref[0, 0] = tp
    part_ref[0, 1] = sp
    part_ref[0, 2] = sl
    part_ref[0, 5] = lsp
    part_ref[0, 6] = ls


def run_core(own, dlo, dhi, hlo, hhi, lab, ldlo, ldhi, lhlo, lhhi, prob, lsk):
    classes, depth, height, wd = prob.shape
    planes = depth + 2 * HALO
    lplanes = depth + 2 * LHALO
    args = (own, dlo, dhi, hlo, hhi, lab, ldlo, ldhi, lhlo, lhhi, prob, lsk)

    def spec(v):
        return pl.BlockSpec((1,) + v.shape[1:], lambda k: (k,) + (0,) * (len(v.shape) - 1))

    full = jax.ShapeDtypeStruct(prob.shape, jnp.float32)
    part = jax.ShapeDtypeStruct((classes, 7, 8, wd), jnp.float32)
    n = ITERS + 1
    return pl.pallas_call(
        core,
        grid=(classes,),
        in_specs=[spec(v) for v in args],
        out_specs=[spec(full), spec(full), spec(part)],
        out_shape=[full, full, part],
        scratch_shapes=[
            pltpu.VMEM((n + 1, planes, ROWS, wd), jnp.float32),
            pltpu.VMEM((n, planes, ROWS, wd), jnp.float32),
            pltpu.VMEM((n, lplanes, ROWS, wd), jnp.float32),
            pltpu.VMEM((n, lplanes, ROWS, wd), jnp.float32),
            pltpu.VMEM((n, lplanes, ROWS, wd), jnp.float32),
            pltpu.VMEM((2, 2, lplanes, ROWS, wd), jnp.float32),
            pltpu.VMEM((lplanes, ROWS, wd), jnp.float32),
        ],
        compiler_params=pltpu.CompilerParams(vmem_limit_bytes=56 * 2**20),
        name="skeleton",
    )(*args)


def all_sum(value):
    for axis in ("height", "depth"):
        n = lax.axis_size(axis)
        spread = jnp.broadcast_to(value[None], (n,) + value.shape)
        value = jnp.sum(lax.all_to_all(spread, axis, 0, 0, tiled=True), axis=0)
    return value


def per_device(features, head_weight, head_bias, labels, label_skeleton):
    classes, channels = head_weight.shape
    _, block_d, block_h, wd = features.shape
    total_cells = block_d * lax.axis_size("depth") * block_h * lax.axis_size("height") * wd
    labf = labels.astype(jnp.float32)
    ldlo, ldhi = exchange(labf, 1, LHALO, "depth")
    ltall = jnp.concatenate([ldlo, labf, ldhi], axis=1)
    lhlo, lhhi = exchange(ltall, 2, LHALO, "height")
    logits = jnp.einsum("kc,cdhw->kdhw", head_weight, features, preferred_element_type=jnp.float32)
    logits = logits + head_bias[:, None, None, None]
    prob = jax.nn.sigmoid(logits)
    own = jnp.exp(-prob / TAU)
    dlo, dhi = exchange(own, 1, HALO, "depth")
    tall = jnp.concatenate([dlo, own, dhi], axis=1)
    hlo, hhi = exchange(tall, 2, HALO, "height")
    ga, gb, part = run_core(
        own, dlo, dhi, hlo, hhi, labf, ldlo, ldhi, lhlo, lhhi, prob, label_skeleton
    )
    lskf = label_skeleton.astype(jnp.float32)
    slope = prob * (1.0 - prob)
    fields = jnp.stack([slope * labf, slope, slope * ga, slope * gb, slope * lskf], axis=1)
    high = fields.astype(jnp.bfloat16)
    low = lax.optimization_barrier((fields - high.astype(jnp.float32)).astype(jnp.bfloat16))
    heads = jnp.einsum("kfdhw,cdhw->kfc", high, features, preferred_element_type=jnp.float32)
    heads = heads + jnp.einsum("kfdhw,cdhw->kfc", low, features, preferred_element_type=jnp.float32)
    local = jnp.concatenate(
        [
            heads.reshape(-1),
            jnp.sum(fields, axis=(2, 3, 4)).reshape(-1),
            jnp.sum(part, axis=(2, 3)).reshape(-1),
            jnp.zeros((-classes * (5 * (channels + 1) + 7) % 1024,), jnp.float32),
        ]
    ).reshape(-1, 128)
    whole = all_sum(local).reshape(-1)
    cut = classes * 5 * channels
    heads = whole[:cut].reshape(classes, 5, channels)
    biases = whole[cut : cut + classes * 5].reshape(classes, 5)
    totals = whole[cut + classes * 5 : cut + classes * 12].reshape(classes, 7).T
    loss = jnp.sum(class_term(totals)) / classes
    scale = total_cells / classes
    dtot = jax.grad(lambda t: jnp.sum(class_term(t)))(totals) * scale
    coef = jnp.stack([dtot[0], dtot[1], dtot[3], dtot[4], dtot[5]])
    grad_w = jnp.sum(coef.T[:, :, None] * heads, axis=1)
    grad_b = jnp.sum(coef.T * biases, axis=1)
    c = coef[:, :, None, None, None]
    dlogit = slope * (c[0] * labf + c[1] + c[2] * ga + c[3] * gb + c[4] * lskf)
    grad_features = sum(
        head_weight[k].astype(jnp.float32)[:, None, None, None] * dlogit[k][None] for k in range(classes)
    ).astype(jnp.bfloat16)
    rms = jnp.sqrt(
        (jnp.sum(grad_w * grad_w) + jnp.sum(grad_b * grad_b)) / (classes * channels + classes)
        + 1e-06
    )
    return (loss, grad_features, grad_w / rms, grad_b / rms)


def solution(mesh):
    return jax.shard_map(
        per_device,
        mesh=mesh,
        in_specs=(
            P(None, "depth", "height", None),
            P(),
            P(),
            P(None, "depth", "height", None),
            P(None, "depth", "height", None),
        ),
        out_specs=(P(), P(None, "depth", "height", None), P(), P()),
        check_vma=False,
    )
```

profile of v0, /device:TPU:1, one launch (start us, length us, event | category | flops | bytes accessed | tf_op | source)
XLA Modules:
  0.0 176.6 jit_solution(397831627579240904)
XLA Ops:
  0.7 3.8 %fusion.6 = f32[3,12,32,128]{3,0,2,1:T(4,128)S(1)} fusion(bf16[32,12,32,128]{3,2,1,0:T(8,128)(2,1)} %param.5, bf16[3,32]{1,0:T(4,128)(2,1)} %param.6), kind=kOutput, calls=%fused_computation.8 | convolution fusion | flops 9437184 | bytes 3735744 | tf_op jit(solution)/shard_map/kc,cdhw->kdhw/dot_general | solution.py:272
  5.0 4.1 %collective-permute-start = (f32[3,10,32,128]{3,2,1,0:T(8,128)S(1)}, f32[3,10,32,128]{3,2,1,0:T(8,128)S(1)}, u32[]{:S(2)}, u32[]{:S(2)}) collective-permute-start(f32[3,10,32,128]{3,2,1,0:T(8,128)S(1)} %get-tuple-element.43), channel_id=1, source_target_pairs={{0,8},{8,16},{16,24},{24,32},{32,40},{40,48},{48,56},{56,64},{64,7... | collective-permute-start | bytes 1474568 | tf_op jit(solution)/shard_map/ppermute | solution.py:32
  9.0 1.3 collective-permute-start.1
  10.4 4.0 %collective-permute-start.4 = (f32[3,5,32,128]{3,2,1,0:T(8,128)S(1)}, f32[3,5,32,128]{3,2,1,0:T(8,128)S(1)}, u32[]{:S(2)}, u32[]{:S(2)}) collective-permute-start(f32[3,5,32,128]{3,2,1,0:T(8,128)S(1)} %get-tuple-element.41), channel_id=1, source_target_pairs={{0,8},{8,16},{16,24},{24,32},{32,40},{40,48},{48,56},{56,64},{64,7... | collective-permute-start | bytes 737288 | tf_op jit(solution)/shard_map/ppermute | solution.py:32
  14.4 1.3 collective-permute-start.5
  15.7 3.1 %collective-permute-done.e_dlo = f32[3,10,32,128]{3,2,1,0:T(8,128)S(1)} collective-permute-done((f32[3,10,32,128]{3,2,1,0:T(8,128)S(1)}, f32[3,10,32,128]{3,2,1,0:T(8,128)S(1)}, u32[]{:S(2)}, u32[]{:S(2)}) %collective-permute-start) | collective-permute-done | bytes 491552 | tf_op jit(solution)/shard_map/ppermute | solution.py:32
  18.9 3.8 %collective-permute-done.1.e_dhi = f32[3,10,32,128]{3,2,1,0:T(8,128)S(1)} collective-permute-done((f32[3,10,32,128]{3,2,1,0:T(8,128)S(1)}, f32[3,10,32,128]{3,2,1,0:T(8,128)S(1)}, u32[]{:S(2)}, u32[]{:S(2)}) %collective-permute-start.1) | collective-permute-done | bytes 491552 | tf_op jit(solution)/shard_map/ppermute | solution.py:32
  23.6 6.3 %collective-permute-start.2 = (f32[3,32,10,128]{3,1,2,0:T(8,128)S(1)}, f32[3,32,10,128]{3,1,2,0:T(8,128)S(1)}, u32[]{:S(2)}, u32[]{:S(2)}) collective-permute-start(f32[3,32,10,128]{3,1,2,0:T(8,128)S(1)} %copy.34), channel_id=1, source_target_pairs={{0,1},{1,2},{2,3},{3,4},{4,5},{5,6},{6,7},{8,9},{9,10},{10,11},{11... | collective-permute-start | bytes 1474568 | tf_op jit(solution)/shard_map/ppermute | solution.py:32
  30.1 1.9 %collective-permute-start.3 = (f32[3,32,10,128]{3,1,2,0:T(8,128)S(1)}, f32[3,32,10,128]{3,1,2,0:T(8,128)S(1)}, u32[]{:S(2)}, u32[]{:S(2)}) collective-permute-start(f32[3,32,10,128]{3,1,2,0:T(8,128)S(1)} %copy.35), channel_id=1, source_target_pairs={{1,0},{2,1},{3,2},{4,3},{5,4},{6,5},{7,6},{9,8},{10,9},{11,10},{12... | collective-permute-start | bytes 1474568 | tf_op jit(solution)/shard_map/ppermute | solution.py:32
  32.2 3.6 %collective-permute-start.6 = (f32[3,22,5,128]{3,2,1,0:T(8,128)S(1)}, f32[3,22,5,128]{3,2,1,0:T(8,128)S(1)}, u32[]{:S(2)}, u32[]{:S(2)}) collective-permute-start(f32[3,22,5,128]{3,2,1,0:T(8,128)S(1)} %get-tuple-element.36), channel_id=1, source_target_pairs={{0,1},{1,2},{2,3},{3,4},{4,5},{5,6},{6,7},{8,9},{9,10},{10,11},{11... | collective-permute-start | bytes 506888 | tf_op jit(solution)/shard_map/ppermute | solution.py:32
  35.8 2.1 %collective-permute-start.7 = (f32[3,22,5,128]{3,2,1,0:T(8,128)S(1)}, f32[3,22,5,128]{3,2,1,0:T(8,128)S(1)}, u32[]{:S(2)}, u32[]{:S(2)}) collective-permute-start(f32[3,22,5,128]{3,2,1,0:T(8,128)S(1)} %get-tuple-element.35), channel_id=1, source_target_pairs={{1,0},{2,1},{3,2},{4,3},{5,4},{6,5},{7,6},{9,8},{10,9},{11,10},{12... | collective-permute-start | bytes 506888 | tf_op jit(solution)/shard_map/ppermute | solution.py:32
  38.0 1.5 copy.36.e_hlo
  40.3 1.2 copy.37.e_hhi
  41.5 2.1 %collective-permute-done.7.l_hhi = f32[3,22,5,128]{3,2,1,0:T(8,128)S(1)} collective-permute-done((f32[3,22,5,128]{3,2,1,0:T(8,128)S(1)}, f32[3,22,5,128]{3,2,1,0:T(8,128)S(1)}, u32[]{:S(2)}, u32[]{:S(2)}) %collective-permute-start.7) | collective-permute-done | bytes 168992 | tf_op jit(solution)/shard_map/ppermute | solution.py:32
  44.3 75.8 %skeleton.1 = (f32[3,12,32,128]{3,2,1,0:T(8,128)}, f32[3,12,32,128]{3,2,1,0:T(8,128)}, f32[3,7,8,128]{3,2,1,0:T(8,128)}) custom-call(f32[3,12,32,128]{3,2,1,0:T(8,128)} %copy-done.2, f32[3,10,32,128]{3,2,1,0:T(8,128)} %copy-done.11, f32[3,10,32,128]{3,2,1,0:T(8,128)} %copy-done.12, f32[3,32,10,128]{3,2,1,0:T(8,128)} %copy.36.e_hlo, ...), custom_call_target="tpu_custom_call" | custom-call | tf_op jit(solution)/shard_map/skeleton/pallas_call | solution.py:236
  120.2 1.2 bitcast_dynamic-update-slice_fusion.2
  121.5 1.2 bitcast_dynamic-update-slice_fusion.1
  123.7 0.9 copy-done.8
  124.7 4.2 %fusion.10 = f32[3,5,32]{2,1,0:T(8,128)S(1)} fusion(bf16[32,12,32,128]{3,2,1,0:T(8,128)(2,1)S(1)} %copy-done.8, bf16[3,5,12,32,128]{4,3,2,0,1:T(8,128)(2,1)S(1)} %get-tuple-element.29), kind=kOutput, calls=%fused_computation.13 | convolution fusion | flops 47185920 | bytes 4622208 | tf_op jit(solution)/shard_map/kfdhw,cdhw->kfc/dot_general | solution.py:287
  128.9 4.3 %fusion.20 = f32[3,5,32]{2,1,0:T(8,128)S(1)} fusion(f32[3,5,32]{2,1,0:T(8,128)S(1)} %fusion.10, bf16[32,12,32,128]{3,2,1,0:T(8,128)(2,1)S(1)} %copy-done.8, bf16[3,5,12,32,128]{4,3,2,0,1:T(8,128)(2,1)S(1)} %get-tuple-element.28), kind=kOutput, calls=%fused_computation.15 | convolution fusion | flops 47186400 | bytes 4624128 | tf_op jit(solution)/shard_map/kfdhw,cdhw->kfc/dot_general | solution.py:288
  133.8 8.6 %all_to_all.10 = f32[8,8,128]{2,1,0:T(8,128)S(1)} all-to-all(f32[8,8,128]{2,1,0:T(8,128)S(1)} %broadcast_in_dim.10), channel_id=1, replica_groups=mesh['depth'=32,'height'=8] {'height'}, dimensions={0} | all-to-all | bytes 65536 | tf_op jit(solution)/shard_map/all_to_all | solution.py:260
  143.1 13.0 %all-to-all-start.1 = ((f32[32,8,128]{2,1,0:T(8,128)}), f32[32,8,128]{2,1,0:T(8,128)S(1)}, u32[]{:S(2)}, u32[]{:S(2)}) async-start(f32[32,8,128]{2,1,0:T(8,128)} %broadcast_in_dim.11), calls=%async_computation.1 | async-start | bytes 262144 | tf_op jit(solution)/shard_map/all_to_all | solution.py:260
  156.1 9.3 %all-to-all-done.1 = f32[32,8,128]{2,1,0:T(8,128)S(1)} async-done(((f32[32,8,128]{2,1,0:T(8,128)}), f32[32,8,128]{2,1,0:T(8,128)S(1)}, u32[]{:S(2)}, u32[]{:S(2)}) %all-to-all-start.1) | async-done | bytes 131104 | tf_op jit(solution)/shard_map/all_to_all | solution.py:260
  172.3 3.2 %add_convert_fusion = bf16[32,12,32,128]{3,2,1,0:T(8,128)(2,1)} fusion(f32[12,32,128]{2,1,0:T(8,128)S(1)} %get-tuple-element.38, f32[32]{0:T(128)S(1)} %get-tuple-element.54, f32[12,32,128]{2,1,0:T(8,128)S(1)} %get-tuple-element.39, f32[32]{0:T(128)S(1)} %get-tuple-element.55, f32[12,32,128]{2,1,0:T(8,128)S(1)} %get-tuple-element.37, f32[32]{0:T(128)S(1)} %get-tuple-element.53), kind=kLoop, calls=%fused_computation | loop fusion | flops 9437184 | bytes 3735936 | tf_op jit(solution)/shard_map/convert_element_type | solution.py:312
  (91 shorter events, 10.5 us)
Async XLA Ops:
  0.6 3.8 %copy-start.19 = (f32[3]{0:T(128)S(1)}, f32[3]{0:T(128)}, u32[]{:S(2)}) copy-start(f32[3]{0:T(128)} %param.7) | copy-start | bytes 40
  0.6 3.8 %copy-start.5 = (s32[3,12,32,128]{3,2,1,0:T(8,128)S(1)}, s32[3,12,32,128]{3,2,1,0:T(8,128)}, u32[]{:S(2)}) copy-start(s32[3,12,32,128]{3,2,1,0:T(8,128)} %param.8) | copy-start | bytes 1769476
  4.7 33.2 %copy-start = (f32[3,12,32,128]{3,2,1,0:T(8,128)}, f32[3,12,32,128]{3,2,1,0:T(8,128)S(1)}, u32[]{:S(2)}) copy-start(f32[3,12,32,128]{3,2,1,0:T(8,128)S(1)} %get-tuple-element.31.p_own) | copy-start | bytes 1769476
  4.8 18.0 %copy-start.2 = (f32[3,12,32,128]{3,2,1,0:T(8,128)}, f32[3,12,32,128]{3,2,1,0:T(8,128)S(1)}, u32[]{:S(2)}) copy-start(f32[3,12,32,128]{3,2,1,0:T(8,128)S(1)} %multiply_exponential_fusion.e_own) | copy-start | bytes 1769476
  5.0 13.9 %collective-permute-start = (f32[3,10,32,128]{3,2,1,0:T(8,128)S(1)}, f32[3,10,32,128]{3,2,1,0:T(8,128)S(1)}, u32[]{:S(2)}, u32[]{:S(2)}) collective-permute-start(f32[3,10,32,128]{3,2,1,0:T(8,128)S(1)} %get-tuple-element.43), channel_id=1, source_target_pairs={{0,8},{8,16},{16,24},{24,32},{32,40},{40,48},{48,56},{56,64},{64,7... | collective-permute-start | bytes 1474568 | tf_op jit(solution)/shard_map/ppermute | solution.py:32
  9.0 13.7 %collective-permute-start.1 = (f32[3,10,32,128]{3,2,1,0:T(8,128)S(1)}, f32[3,10,32,128]{3,2,1,0:T(8,128)S(1)}, u32[]{:S(2)}, u32[]{:S(2)}) collective-permute-start(f32[3,10,32,128]{3,2,1,0:T(8,128)S(1)} %get-tuple-element.42), channel_id=1, source_target_pairs={{8,0},{16,8},{24,16},{32,24},{40,32},{48,40},{56,48},{64,56},{72,6... | collective-permute-start | bytes 1474568 | tf_op jit(solution)/shard_map/ppermute | solution.py:32
  10.4 21.7 %copy-start.3 = (f32[3,12,32,128]{3,2,1,0:T(8,128)}, f32[3,12,32,128]{3,2,1,0:T(8,128)S(1)}, u32[]{:S(2)}) copy-start(f32[3,12,32,128]{3,2,1,0:T(8,128)S(1)} %convert_element_type.48.l_own) | copy-start | bytes 1769476
  10.4 21.7 %collective-permute-start.4 = (f32[3,5,32,128]{3,2,1,0:T(8,128)S(1)}, f32[3,5,32,128]{3,2,1,0:T(8,128)S(1)}, u32[]{:S(2)}, u32[]{:S(2)}) collective-permute-start(f32[3,5,32,128]{3,2,1,0:T(8,128)S(1)} %get-tuple-element.41), channel_id=1, source_target_pairs={{0,8},{8,16},{16,24},{24,32},{32,40},{40,48},{48,56},{56,64},{64,7... | collective-permute-start | bytes 737288 | tf_op jit(solution)/shard_map/ppermute | solution.py:32
  14.4 17.7 %collective-permute-start.5 = (f32[3,5,32,128]{3,2,1,0:T(8,128)S(1)}, f32[3,5,32,128]{3,2,1,0:T(8,128)S(1)}, u32[]{:S(2)}, u32[]{:S(2)}) collective-permute-start(f32[3,5,32,128]{3,2,1,0:T(8,128)S(1)} %get-tuple-element.40), channel_id=1, source_target_pairs={{8,0},{16,8},{24,16},{32,24},{40,32},{48,40},{56,48},{64,56},{72,6... | collective-permute-start | bytes 737288 | tf_op jit(solution)/shard_map/ppermute | solution.py:32
  18.9 4.1 %copy-start.11 = (f32[3,10,32,128]{3,2,1,0:T(8,128)}, f32[3,10,32,128]{3,2,1,0:T(8,128)S(1)}, u32[]{:S(2)}) copy-start(f32[3,10,32,128]{3,2,1,0:T(8,128)S(1)} %collective-permute-done.e_dlo) | copy-start | bytes 1474564
  23.6 14.4 %collective-permute-start.2 = (f32[3,32,10,128]{3,1,2,0:T(8,128)S(1)}, f32[3,32,10,128]{3,1,2,0:T(8,128)S(1)}, u32[]{:S(2)}, u32[]{:S(2)}) collective-permute-start(f32[3,32,10,128]{3,1,2,0:T(8,128)S(1)} %copy.34), channel_id=1, source_target_pairs={{0,1},{1,2},{2,3},{3,4},{4,5},{5,6},{6,7},{8,9},{9,10},{10,11},{11... | collective-permute-start | bytes 1474568 | tf_op jit(solution)/shard_map/ppermute | solution.py:32
  30.1 10.1 %collective-permute-start.3 = (f32[3,32,10,128]{3,1,2,0:T(8,128)S(1)}, f32[3,32,10,128]{3,1,2,0:T(8,128)S(1)}, u32[]{:S(2)}, u32[]{:S(2)}) collective-permute-start(f32[3,32,10,128]{3,1,2,0:T(8,128)S(1)} %copy.35), channel_id=1, source_target_pairs={{1,0},{2,1},{3,2},{4,3},{5,4},{6,5},{7,6},{9,8},{10,9},{11,10},{12... | collective-permute-start | bytes 1474568 | tf_op jit(solution)/shard_map/ppermute | solution.py:32
  32.1 11.5 %copy-start.13 = (f32[3,5,32,128]{3,2,1,0:T(8,128)}, f32[3,5,32,128]{3,2,1,0:T(8,128)S(1)}, u32[]{:S(2)}) copy-start(f32[3,5,32,128]{3,2,1,0:T(8,128)S(1)} %collective-permute-done.4.l_dlo) | copy-start | bytes 737284
  32.1 11.5 %copy-start.14 = (f32[3,5,32,128]{3,2,1,0:T(8,128)}, f32[3,5,32,128]{3,2,1,0:T(8,128)S(1)}, u32[]{:S(2)}) copy-start(f32[3,5,32,128]{3,2,1,0:T(8,128)S(1)} %collective-permute-done.5.l_dhi) | copy-start | bytes 737284
  32.2 9.3 %collective-permute-start.6 = (f32[3,22,5,128]{3,2,1,0:T(8,128)S(1)}, f32[3,22,5,128]{3,2,1,0:T(8,128)S(1)}, u32[]{:S(2)}, u32[]{:S(2)}) collective-permute-start(f32[3,22,5,128]{3,2,1,0:T(8,128)S(1)} %get-tuple-element.36), channel_id=1, source_target_pairs={{0,1},{1,2},{2,3},{3,4},{4,5},{5,6},{6,7},{8,9},{9,10},{10,11},{11... | collective-permute-start | bytes 506888 | tf_op jit(solution)/shard_map/ppermute | solution.py:32
  35.8 7.8 %collective-permute-start.7 = (f32[3,22,5,128]{3,2,1,0:T(8,128)S(1)}, f32[3,22,5,128]{3,2,1,0:T(8,128)S(1)}, u32[]{:S(2)}, u32[]{:S(2)}) collective-permute-start(f32[3,22,5,128]{3,2,1,0:T(8,128)S(1)} %get-tuple-element.35), channel_id=1, source_target_pairs={{1,0},{2,1},{3,2},{4,3},{5,4},{6,5},{7,6},{9,8},{10,9},{11,10},{12... | collective-permute-start | bytes 506888 | tf_op jit(solution)/shard_map/ppermute | solution.py:32
  41.5 78.7 %copy-start.1 = (f32[3,12,32,128]{3,2,1,0:T(8,128)S(1)}, f32[3,12,32,128]{3,2,1,0:T(8,128)}, u32[]{:S(2)}) copy-start(f32[3,12,32,128]{3,2,1,0:T(8,128)} %copy-done) | copy-start | bytes 1769476
  41.5 78.7 %copy-start.7 = (f32[3,5,12,32,128]{4,3,2,0,1:T(8,128)S(1)}, f32[3,5,12,32,128]{4,3,2,0,1:T(8,128)}, u32[]{:S(2)}) copy-start(f32[3,5,12,32,128]{4,3,2,0,1:T(8,128)} %copy-done.6) | copy-start | bytes 8847364
  120.2 2.5 %copy-start.4 = (s32[3,12,32,128]{3,2,1,0:T(8,128)S(1)}, s32[3,12,32,128]{3,2,1,0:T(8,128)}, u32[]{:S(2)}) copy-start(s32[3,12,32,128]{3,2,1,0:T(8,128)} %k_own.1) | copy-start | bytes 1769476
  128.9 4.6 %copy-start.17 = (f32[3,7,8,128]{3,2,1,0:T(8,128)S(1)}, f32[3,7,8,128]{3,2,1,0:T(8,128)}, u32[]{:S(2)}) copy-start(f32[3,7,8,128]{3,2,1,0:T(8,128)} %get-tuple-element.9) | copy-start | bytes 258052
  128.9 27.1 %copy-start.18 = (bf16[3,32]{1,0:T(4,128)(2,1)S(1)}, bf16[3,32]{1,0:T(4,128)(2,1)}, u32[]{:S(2)}) copy-start(bf16[3,32]{1,0:T(4,128)(2,1)} %param.6) | copy-start | bytes 580
  128.9 41.7 %copy-start.9 = (f32[3,12,32,128]{3,2,1,0:T(8,128)S(1)}, f32[3,12,32,128]{3,2,1,0:T(8,128)}, u32[]{:S(2)}) copy-start(f32[3,12,32,128]{3,2,1,0:T(8,128)} %get-tuple-element.7) | copy-start | bytes 1769476
  128.9 41.7 %copy-start.10 = (f32[3,12,32,128]{3,2,1,0:T(8,128)S(1)}, f32[3,12,32,128]{3,2,1,0:T(8,128)}, u32[]{:S(2)}) copy-start(f32[3,12,32,128]{3,2,1,0:T(8,128)} %get-tuple-element.8) | copy-start | bytes 1769476
  143.1 22.3 %all-to-all-start.1 = ((f32[32,8,128]{2,1,0:T(8,128)}), f32[32,8,128]{2,1,0:T(8,128)S(1)}, u32[]{:S(2)}, u32[]{:S(2)}) async-start(f32[32,8,128]{2,1,0:T(8,128)} %broadcast_in_dim.11), calls=%async_computation.1 | async-start | bytes 262144 | tf_op jit(solution)/shard_map/all_to_all | solution.py:260
  (5 other events, 7.8 us)
where the time goes:
time: 177 us
  Pallas kernels  75.8 us (43%)
  starting transfers between devices  37.6 us (21%)
  waiting for transfers between devices  19.2 us (11%)
  matrix products  12.3 us (7%)
  other arithmetic  11.6 us (7%)
  blocking collectives  8.63 us (5%)
  local copies, waits for them, and re-layouts  7.24 us (4%)
  between operations  4.22 us (2%)
    pallas_call x1, Pallas kernels, run_core(): pl.pallas_call(core, grid=(classes,), in_specs=[spec(v) for v in args], o...  75.8 us
    ppermute x8, starting transfers between devices, shift(): return lax.ppermute(value, axis, pairs)  24.6 us
    all_to_all x1, starting transfers between devices, all_sum(): value = jnp.sum(lax.all_to_all(spread, axis, 0, 0, tiled=True), axis=0)  13 us
    ppermute x8, waiting for transfers between devices, shift(): return lax.ppermute(value, axis, pairs)  9.85 us
    all_to_all x1, waiting for transfers between devices, all_sum(): value = jnp.sum(lax.all_to_all(spread, axis, 0, 0, tiled=True), axis=0)  9.33 us
    all_to_all x1, blocking collectives, all_sum(): value = jnp.sum(lax.all_to_all(spread, axis, 0, 0, tiled=True), axis=0)  8.63 us
    dot_general x1, matrix products, per_device(): jnp.einsum('kfdhw,cdhw->kfc', low, features, preferred_element_type=jnp.f...  4.25 us
    dot_general x1, matrix products, per_device(): jnp.einsum('kfdhw,cdhw->kfc', high, features, preferred_element_type=jnp....  4.22 us
  transfers between devices with their start and end apart: 9, of which 5 were waited for; matrix products, arithmetic and copies ran while one was open for 2% of the time, Pallas kernels for 0%

commit v1 on v0

v1 whole, which is shorter than its diff:
```python
import functools

import jax
import jax.numpy as jnp
from jax import lax
from jax.experimental import pallas as pl
from jax.experimental.pallas import tpu as pltpu
from jax.sharding import PartitionSpec as P

ITERS = 3
TAU = 0.1
SHARP = 0.05
ALPHA = 0.3
BETA = 0.7
HALO = 10
LHALO = 5
ROWS = 80
OFF = 24
NB = 4
MXU = 2
FIELDS = 5
EXACT = lax.Precision.HIGHEST
LAST = (((1,), (1,)), ((), ()))


def shift(value, axis, step):
    n = lax.axis_size(axis)
    pairs = [(i, i + step) for i in range(n) if 0 <= i + step < n]
    return lax.ppermute(value, axis, pairs)


def head_kernel(w_ref, b_ref, f_ref, l_ref, p_ref, e_ref, first_ref, last_ref):
    d = pl.program_id(0)
    depth = pl.num_programs(0)
    channels = f_ref.shape[0]
    height = f_ref.shape[2]
    classes = p_ref.shape[0]
    acc = [None] * classes
    for c in range(channels):
        f = f_ref[c, 0].astype(jnp.float32)
        for k in range(classes):
            term = w_ref[k, c] * f
            acc[k] = term if c == 0 else acc[k] + term
    exps, labs = [], []
    for k in range(classes):
        prob = 1.0 / (1.0 + jnp.exp(-(acc[k] + b_ref[k])))
        p_ref[k, 0] = prob
        exps.append(jnp.exp(prob * (-1.0 / TAU)))
        e_ref[k, 0] = exps[k]
        labs.append(l_ref[k, 0].astype(jnp.float32))

    def put(ref, row, values):
        for k in range(classes):
            ref[k, pl.ds(pl.multiple_of(row * height, height), height), :] = values[k]

    @pl.when(d < HALO)
    def _():
        put(first_ref, d, exps)

    @pl.when(d >= depth - HALO)
    def _():
        put(last_ref, d - (depth - HALO), exps)

    @pl.when(d < LHALO)
    def _():
        put(first_ref, HALO + d, labs)

    @pl.when(d >= depth - LHALO)
    def _():
        put(last_ref, HALO + d - (depth - LHALO), labs)


def run_head(weight, bias, features, labels):
    classes, depth, height, wd = labels.shape
    channels = features.shape[0]
    plane = pl.BlockSpec((classes, 1, height, wd), lambda d: (0, d, 0, 0))
    rows = (HALO + LHALO) * height
    strip = pl.BlockSpec((classes, rows, wd), lambda d: (0, 0, 0))
    full = jax.ShapeDtypeStruct(labels.shape, jnp.float32)
    edge = jax.ShapeDtypeStruct((classes, rows, wd), jnp.float32)
    return pl.pallas_call(
        head_kernel,
        grid=(depth,),
        in_specs=[
            pl.BlockSpec(memory_space=pltpu.SMEM),
            pl.BlockSpec(memory_space=pltpu.SMEM),
            pl.BlockSpec((channels, 1, height, wd), lambda d: (0, d, 0, 0)),
            plane,
        ],
        out_specs=[plane, plane, strip, strip],
        out_shape=[full, full, edge, edge],
        compiler_params=pltpu.CompilerParams(vmem_limit_bytes=32 * 2**20),
        name="head",
    )(weight, bias, features, labels)


def side_kernel(e_ref, l_ref, lo_ref, hi_ref, first_ref, last_ref):
    depth, height = e_ref.shape[1], e_ref.shape[2]
    for out, near in ((first_ref, True), (last_ref, False)):
        for p in range(depth + 2 * HALO):
            at = 0 if near else height - HALO
            if p < HALO:
                v = lo_ref[0, pl.ds(p * height + at, HALO), :]
            elif p < HALO + depth:
                v = e_ref[0, p - HALO, pl.ds(at, HALO), :]
            else:
                v = hi_ref[0, pl.ds((p - HALO - depth) * height + at, HALO), :]
            out[0, pl.ds(p * HALO, HALO), :] = v
        base = HALO * (depth + 2 * HALO)
        for p in range(depth + 2 * LHALO):
            at = 0 if near else height - LHALO
            if p < LHALO:
                v = lo_ref[0, pl.ds((HALO + p) * height + at, LHALO), :]
            elif p < LHALO + depth:
                v = l_ref[0, p - LHALO, pl.ds(at, LHALO), :].astype(jnp.float32)
            else:
                v = hi_ref[0, pl.ds((HALO + p - LHALO - depth) * height + at, LHALO), :]
            out[0, pl.ds(base + p * LHALO, LHALO), :] = v


def by_class(v):
    return pl.BlockSpec((1,) + v.shape[1:], lambda k: (k,) + (0,) * (len(v.shape) - 1))


def run_side(own, labels, lo, hi):
    classes, depth, height, wd = own.shape
    rows = HALO * (depth + 2 * HALO) + LHALO * (depth + 2 * LHALO)
    edge = jax.ShapeDtypeStruct((classes, rows, wd), jnp.float32)
    args = (own, labels, lo, hi)
    return pl.pallas_call(
        side_kernel,
        grid=(classes,),
        in_specs=[by_class(v) for v in args],
        out_specs=[by_class(edge)] * 2,
        out_shape=[edge, edge],
        compiler_params=pltpu.CompilerParams(vmem_limit_bytes=32 * 2**20),
        name="side",
    )(*args)


def wide_sums(values, lane, band):
    rows, width = values[0].shape
    out = []
    if MXU:
        s = jnp.concatenate(values[:MXU], axis=0)
        high = s.astype(jnp.bfloat16)
        low = (s - high.astype(jnp.float32)).astype(jnp.bfloat16)
        s = jnp.dot(jnp.concatenate([high, low], axis=1), band, preferred_element_type=jnp.float32)
        out = [s[i * rows : (i + 1) * rows] for i in range(MXU)]
    for s in values[MXU:]:
        left = jnp.where(lane == 0, 0.0, pltpu.roll(s, 1, 1))
        right = jnp.where(lane == width - 1, 0.0, pltpu.roll(s, width - 1, 1))
        out.append(s + left + right)
    return out


def boxes(load, d, r0, nr, lane, band):
    h = []
    for i in range(NB + 2):
        h.append(load(d + i - 1, r0 - 1, nr) + load(d + i - 1, r0, nr) + load(d + i - 1, r0 + 1, nr))
    out = []
    for i in range(0, NB, 2):
        mid = h[i + 1] + h[i + 2]
        out.append(h[i] + mid)
        out.append(mid + h[i + 3])
    return wide_sums(out, lane, band)


def sweep(first, last, body):
    for i in range(first, last, NB):
        body(min(i, last - NB))


def core_kernel(
    f_ref, e_own, e_lo, e_hi, e_left, e_right, l_own, p_own, k_own,
    x_ref, sum_ref,
    E, R, X, U, V, Q, L, S, A, T, B,
):
    k = pl.program_id(0)
    depth, height, wd = p_own.shape[1:]
    planes = depth + 2 * HALO
    lplanes = depth + 2 * LHALO
    base = HALO - LHALO
    side = HALO * planes

    @pl.when(k == 0)
    def _():
        row = lax.broadcasted_iota(jnp.int32, (2 * wd, wd), 0)
        col = lax.broadcasted_iota(jnp.int32, (2 * wd, wd), 1)
        near = jnp.abs(jnp.where(row < wd, row, row - wd) - col) <= 1
        B[...] = jnp.where(near, 1.0, 0.0).astype(jnp.bfloat16)

    E[0, :, OFF - HALO - 8 : OFF - HALO, :] = jnp.zeros((planes, 8, wd), jnp.float32)
    E[0, :, OFF + height + HALO : OFF + height + HALO + 8, :] = jnp.zeros((planes, 8, wd), jnp.float32)
    E[0, HALO : HALO + depth, OFF : OFF + height, :] = e_own[0]
    for p in range(HALO):
        E[0, p, OFF : OFF + height, :] = e_lo[0, p * height : (p + 1) * height, :]
        E[0, HALO + depth + p, OFF : OFF + height, :] = e_hi[0, p * height : (p + 1) * height, :]
    for p in range(planes):
        E[0, p, OFF - HALO : OFF, :] = e_left[0, p * HALO : (p + 1) * HALO, :]
        E[0, p, OFF + height : OFF + height + HALO, :] = e_right[0, p * HALO : (p + 1) * HALO, :]
    L[:, OFF - 8 : OFF - LHALO, :] = jnp.zeros((lplanes, 8 - LHALO, wd), jnp.float32)
    L[:, OFF + height + LHALO : OFF + height + 8, :] = jnp.zeros((lplanes, 8 - LHALO, wd), jnp.float32)
    L[LHALO : LHALO + depth, OFF : OFF + height, :] = l_own[0].astype(jnp.float32)
    for p in range(LHALO):
        at = (HALO + p) * height
        L[p, OFF : OFF + height, :] = e_lo[0, at : at + height, :]
        L[LHALO + depth + p, OFF : OFF + height, :] = e_hi[0, at : at + height, :]
    for p in range(lplanes):
        at = side + p * LHALO
        L[p, OFF - LHALO : OFF, :] = e_left[0, at : at + LHALO, :]
        L[p, OFF + height : OFF + height + LHALO, :] = e_right[0, at : at + LHALO, :]

    band = B[...]
    w0, wn = OFF - 8, height + 16
    lane = lax.broadcasted_iota(jnp.int32, (wn, wd), 1)
    lane_big = lax.broadcasted_iota(jnp.int32, (wn + 16, wd), 1)
    lane_own = lax.broadcasted_iota(jnp.int32, (height, wd), 1)

    for j in range(ITERS + 1):
        r0, nr, ln = (w0 - 8, wn + 16, lane_big) if j == 0 else (w0, wn, lane)

        def erode(d, j=j, r0=r0, nr=nr, ln=ln):
            outs = boxes(lambda a, b, n: E[j, a, pl.ds(b, n), :], d, r0, nr, ln, band)
            for i, s in enumerate(outs):
                live = E[0, d + i, pl.ds(r0, nr), :] > 0.0
                E[j + 1, d + i, pl.ds(r0, nr), :] = jnp.where(live, s, 0.0)
                R[j, d + i, pl.ds(r0, nr), :] = jnp.where(live, 1.0 / s, 0.0)

        sweep(j + 1, planes - j - 1, erode)

    for j in range(ITERS + 1):

        def dilate(d, j=j):
            outs = boxes(lambda a, b, n: R[j, a, pl.ds(b, n), :], d, w0, wn, lane, band)
            for i, s in enumerate(outs):
                live = E[0, d + i, pl.ds(w0, wn), :] > 0.0
                rd = 1.0 / s
                t = rd / E[j, d + i, pl.ds(w0, wn), :]
                U[j, d + i - base, pl.ds(w0, wn), :] = jnp.where(live, rd, 0.0)
                X[j, d + i - base, pl.ds(w0, wn), :] = jnp.where(live, t * t, 0.0)

        sweep(base, planes - base, dilate)

    row = lax.broadcasted_iota(jnp.int32, (wn, wd), 0)
    inner = jnp.where((row >= OFF - w0) & (row < OFF - w0 + height), 1.0, 0.0)

    def point(d, carry):
        rows = pl.ds(w0, wn)
        x = [X[j, d, rows, :] for j in range(ITERS + 1)]
        opx = [1.0 + v for v in x]
        delta = [SHARP * jnp.log(v) for v in opx]
        skel = delta[0]
        om, su = [None], [None]
        for j in range(1, ITERS + 1):
            om.append(1.0 - skel)
            e = jnp.exp(delta[j] * om[j] * (1.0 / SHARP))
            ope = 1.0 + e
            skel = skel + SHARP * jnp.log(ope)
            su.append(e / ope)
        lab = L[d, rows, :]
        g = None
        for j in range(ITERS, -1, -1):
            gv = x[j] / opx[j]
            if j:
                gv = gv * su[j] * om[j]
            if g is not None:
                gv = gv * g
            if j:
                keep = 1.0 - su[j] * delta[j]
                g = keep if g is None else g * keep
            u = gv * U[j, d, rows, :]
            X[j, d, rows, :] = gv
            U[j, d, rows, :] = u
            V[j, d, rows, :] = u * lab
        own = jnp.where((d >= LHALO) & (d < LHALO + depth), 1.0, 0.0)
        skel = skel * (inner * own)
        return carry[0] + skel * lab, carry[1] + skel

    zero = jnp.zeros((wn, wd), jnp.float32)
    sky, sk = lax.fori_loop(0, lplanes, point, (zero, zero), unroll=2)

    for j in range(ITERS + 1, 0, -1):
        now, nxt = j % 2, (j + 1) % 2

        def back(d, j=j, now=now, nxt=nxt):
            b = d - base
            for which, src in ((0, V), (1, U)):
                du = boxes(lambda a, c, n: src[j - 1, a, pl.ds(c, n), :], b, w0, wn, lane, band)
                if j <= ITERS:
                    dq = boxes(lambda a, c, n: Q[which, nxt, a, pl.ds(c, n), :], b, w0, wn, lane, band)
                for i in range(NB):
                    r = R[j - 1, d + i, pl.ds(w0, wn), :]
                    v = -r * du[i]
                    if j <= ITERS:
                        live = E[0, d + i, pl.ds(w0, wn), :] > 0.0
                        gv = X[j, b + i, pl.ds(w0, wn), :]
                        if which == 0:
                            gv = gv * L[b + i, pl.ds(w0, wn), :]
                        v = jnp.where(live, r * (gv + v) + dq[i], 0.0)
                    else:
                        v = r * v
                    Q[which, now, b + i, pl.ds(w0, wn), :] = v

        sweep(HALO - j, planes - HALO + j, back)

    sums = [jnp.zeros((height, wd), jnp.float32) for _ in range(5 + FIELDS)]

    def last(d):
        b = d - base
        o = d - HALO
        grads = [
            boxes(lambda a, c, n: Q[which, 1, a, pl.ds(c, n), :], b, OFF, height, lane_own, band)
            for which in range(2)
        ]
        for i in range(NB):
            e = E[0, d + i, pl.ds(OFF, height), :]
            gv = X[0, b + i, pl.ds(OFF, height), :]
            prob = p_own[0, o + i]
            lab = L[b + i, pl.ds(OFF, height), :]
            lsk = k_own[0, o + i].astype(jnp.float32)
            slope = prob * (1.0 - prob)
            fields = [
                slope * lab,
                slope,
                slope * (gv * lab + e * grads[0][i]),
                slope * (gv + e * grads[1][i]),
                slope * lsk,
            ]
            parts = [prob * lab, prob, lab, lsk * prob, lsk] + fields
            for n, v in enumerate(parts):
                sums[n] = sums[n] + v
            for f, v in enumerate(fields):
                x_ref[0, f, o + i] = v
                high = v.astype(jnp.bfloat16)
                low = (v - high.astype(jnp.float32)).astype(jnp.bfloat16)
                for t in range(height // 16):
                    at = pl.ds(pl.multiple_of((k * FIELDS + f) * 32, 32), 16)
                    S[o + i, at, t * wd : (t + 1) * wd] = high[16 * t : 16 * t + 16]
                    at = pl.ds(pl.multiple_of((k * FIELDS + f) * 32, 32) + 16, 16)
                    S[o + i, at, t * wd : (t + 1) * wd] = low[16 * t : 16 * t + 16]

    sweep(HALO, HALO + depth, last)
    tp, sp, sl, lsp, ls = sums[:5]

    def stack(values):
        values = [jnp.sum(v, axis=0, keepdims=True) for v in values]
        values += [jnp.zeros((1, wd), jnp.float32)] * (8 - len(values))
        return jnp.concatenate(values, axis=0)

    col = lax.broadcasted_iota(jnp.int32, (wd, wd // 4), 1)

    def column(n):
        return jnp.where(col == n, 1.0, 0.0)

    here = jnp.dot(stack([tp, sp, sl, sky, sk, lsp, ls]), column(k), precision=EXACT)
    here = here + jnp.dot(stack(sums[5:]), column(pl.num_programs(0) + k), precision=EXACT)

    @pl.when(k == 0)
    def _():
        T[...] = here

    @pl.when(k > 0)
    def _():
        T[...] = T[...] + here

    @pl.when(k == pl.num_programs(0) - 1)
    def _():
        channels = f_ref.shape[0]
        cols = S.shape[1]

        def plane(d, carry):
            f = jnp.concatenate(
                [f_ref[:, d, 16 * t : 16 * t + 16, :].reshape(channels * 16, wd) for t in range(height // 16)],
                axis=1,
            )
            got = lax.dot_general(f, S[d], LAST, preferred_element_type=jnp.float32)

            @pl.when(d == 0)
            def _():
                A[...] = got

            @pl.when(d > 0)
            def _():
                A[...] = A[...] + got

            return carry

        lax.fori_loop(0, depth, plane, 0)
        h = lax.broadcasted_iota(jnp.int32, (channels, 16, cols), 1)
        g = lax.broadcasted_iota(jnp.int32, (channels, 16, cols), 2) % 16
        m = jnp.sum(jnp.where(h == g, A[...].reshape(channels, 16, cols), 0.0), axis=1)
        item = lax.broadcasted_iota(jnp.int32, (8, cols), 0)
        at = lax.broadcasted_iota(jnp.int32, (8, cols), 1) // 32
        heads = []
        for n in range(cols // 32 // FIELDS):
            pick = jnp.where((at == n * FIELDS + item) & (item < FIELDS), 1.0, 0.0)
            heads.append(lax.dot_general(pick, m, LAST, precision=EXACT))
        whole = jnp.concatenate(heads + [T[...]], axis=1)
        for n in range(sum_ref.shape[0]):
            sum_ref[n] = whole


def run_core(copies, features, own, lo, hi, left, right, labels, prob, lsk):
    classes, depth, height, wd = prob.shape
    channels = features.shape[0]
    planes = depth + 2 * HALO
    lplanes = depth + 2 * LHALO
    args = (own, lo, hi, left, right, labels, prob, lsk)
    n = ITERS + 1
    cols = classes * FIELDS * 32
    fields = jax.ShapeDtypeStruct((classes, FIELDS, depth, height, wd), jnp.float32)
    sums = jax.ShapeDtypeStruct((copies, 8, wd), jnp.float32)
    return pl.pallas_call(
        core_kernel,
        grid=(classes,),
        in_specs=[pl.BlockSpec(features.shape, lambda k: (0, 0, 0, 0))] + [by_class(v) for v in args],
        out_specs=[by_class(fields), pl.BlockSpec(sums.shape, lambda k: (0, 0, 0))],
        out_shape=[fields, sums],
        scratch_shapes=[
            pltpu.VMEM((n + 1, planes, ROWS, wd), jnp.float32),
            pltpu.VMEM((n, planes, ROWS, wd), jnp.float32),
            pltpu.VMEM((n, lplanes, ROWS, wd), jnp.float32),
            pltpu.VMEM((n, lplanes, ROWS, wd), jnp.float32),
            pltpu.VMEM((n, lplanes, ROWS, wd), jnp.float32),
            pltpu.VMEM((2, 2, lplanes, ROWS, wd), jnp.float32),
            pltpu.VMEM((lplanes, ROWS, wd), jnp.float32),
            pltpu.VMEM((depth, cols, height // 16 * wd), jnp.bfloat16),
            pltpu.VMEM((channels * 16, cols), jnp.float32),
            pltpu.VMEM((8, wd // 4), jnp.float32),
            pltpu.VMEM((2 * wd, wd), jnp.bfloat16),
        ],
        compiler_params=pltpu.CompilerParams(vmem_limit_bytes=60 * 2**20),
        name="core",
    )(features, *args)


def tail_kernel(cells, w_ref, s_ref, x_ref, g_ref, out_ref, C):
    classes = x_ref.shape[0]
    channels = g_ref.shape[0]
    quarter = s_ref.shape[2] // 4
    wd = s_ref.shape[2]

    @pl.when(pl.program_id(0) == 0)
    def _():
        total = jnp.sum(s_ref[...], axis=0)
        tp, sp, sl, sky, sk, lsp, ls = [jnp.broadcast_to(total[i : i + 1], total.shape) for i in range(7)]
        prec = (sky + 1.0) / (sk + 1.0)
        sens = (lsp + 1.0) / (ls + 1.0)
        both = prec + sens
        cldice = 1.0 - 2.0 * prec * sens / both
        bottom = tp + ALPHA * (sp - tp) + BETA * (sl - tp) + 1.0
        tversky = (tp + 1.0) / bottom
        term = cldice + 1.0 - tversky
        scale = cells / classes
        by_prec = -2.0 * (sens / both) * (sens / both) * scale
        by_sens = -2.0 * (prec / both) * (prec / both) * scale
        by_sky = by_prec / (sk + 1.0)
        by_sk = -by_sky * prec
        by_lsp = by_sens / (ls + 1.0)
        by_sp = scale * ALPHA * tversky / bottom
        by_tp = scale * (tversky * (1.0 - ALPHA - BETA) - 1.0) / bottom
        lane = lax.broadcasted_iota(jnp.int32, total.shape, 1)
        item = lax.broadcasted_iota(jnp.int32, total.shape, 0)
        mult = jnp.zeros_like(total)
        loss = jnp.zeros_like(total)
        for k in range(classes):
            mine = (lane // quarter == k) | (lane == classes * (quarter + 1) + k)
            spot = lane == classes * quarter + k

            def pick(v):
                return jnp.sum(jnp.where(spot, v, 0.0), axis=1, keepdims=True)

            for f, v in enumerate((by_tp, by_sp, by_sky, by_sk, by_lsp)):
                v = jnp.broadcast_to(pick(v), total.shape)
                C[k, f] = v
                mult = jnp.where(mine & (item == f), v, mult)
            loss = loss + pick(term) * (1.0 / classes)
        grad = jnp.sum(jnp.where(item < FIELDS, total * mult, 0.0), axis=0, keepdims=True)
        square = jnp.sum(grad * grad, axis=1, keepdims=True)
        rms = jnp.sqrt(square / (classes * channels + classes) + 1e-06)
        out_ref[...] = jnp.where(item == 0, grad / rms, loss)

    height = x_ref.shape[3]
    for p in range(x_ref.shape[2]):
        for t in range(height // 16):
            rows = slice(16 * t, 16 * t + 16)
            dlogit = []
            for k in range(classes):
                v = None
                for f in range(FIELDS):
                    c = jnp.concatenate([C[k, f]] * 2, axis=0)
                    term = c * x_ref[k, f, p, rows, :]
                    v = term if v is None else v + term
                dlogit.append(v)
            for c in range(channels):
                v = None
                for k in range(classes):
                    term = w_ref[k, c] * dlogit[k]
                    v = term if v is None else v + term
                g_ref[c, p, rows, :] = v.astype(jnp.bfloat16)


def run_tail(cells, weight, sums, fields):
    classes, n, depth, height, wd = fields.shape
    channels = weight.shape[1]
    step = 2
    return pl.pallas_call(
        functools.partial(tail_kernel, cells),
        grid=(depth // step,),
        in_specs=[
            pl.BlockSpec(memory_space=pltpu.SMEM),
            pl.BlockSpec(sums.shape, lambda d: (0, 0, 0)),
            pl.BlockSpec((classes, n, step, height, wd), lambda d: (0, 0, d, 0, 0)),
        ],
        out_specs=[
            pl.BlockSpec((channels, step, height, wd), lambda d: (0, d, 0, 0)),
            pl.BlockSpec((8, wd), lambda d: (0, 0)),
        ],
        out_shape=[
            jax.ShapeDtypeStruct((channels, depth, height, wd), jnp.bfloat16),
            jax.ShapeDtypeStruct((8, wd), jnp.float32),
        ],
        scratch_shapes=[pltpu.VMEM((classes, FIELDS, 8, wd), jnp.float32)],
        compiler_params=pltpu.CompilerParams(vmem_limit_bytes=32 * 2**20),
        name="tail",
    )(weight, sums, fields)


def per_device(features, head_weight, head_bias, labels, label_skeleton):
    classes, channels = head_weight.shape
    _, block_d, block_h, wd = features.shape
    cells = block_d * lax.axis_size("depth") * block_h * lax.axis_size("height") * wd
    weight = head_weight.astype(jnp.float32)
    prob, own, first, last = run_head(weight, head_bias, features, labels)
    lo, hi = shift(last, "depth", 1), shift(first, "depth", -1)
    first, last = run_side(own, labels, lo, hi)
    left, right = shift(last, "height", 1), shift(first, "height", -1)
    fields, local = run_core(
        lax.axis_size("height"), features, own, lo, hi, left, right, labels, prob, label_skeleton
    )
    part = jnp.sum(lax.all_to_all(local, "height", 0, 0, tiled=True), axis=0)
    spread = jnp.broadcast_to(part[None], (lax.axis_size("depth"),) + part.shape)
    parts = lax.all_to_all(spread, "depth", 0, 0, tiled=True)
    grad_features, small = run_tail(cells, weight, parts, fields)
    n = classes * channels
    return (
        small[1, 0],
        grad_features,
        small[0, :n].reshape(classes, channels),
        small[0, n + classes : n + 2 * classes],
    )


def solution(mesh):
    return jax.shard_map(
        per_device,
        mesh=mesh,
        in_specs=(
            P(None, "depth", "height", None),
            P(),
            P(),
            P(None, "depth", "height", None),
            P(None, "depth", "height", None),
        ),
        out_specs=(P(), P(None, "depth", "height", None), P(), P()),
        check_vma=False,
    )
```

time: 177 us -> 124 us (0.70)
  Pallas kernels: 75.8 us -> 42.4 us
  starting transfers between devices: 37.6 us -> 12.1 us
  blocking collectives: 8.63 us -> 30.9 us
  matrix products: 12.3 us -> 0 us
  other arithmetic: 11.6 us -> 0.69 us
  waiting for transfers between devices: 19.2 us -> 27.7 us
  between operations: 4.22 us -> 0.71 us
    pallas_call x1 -> x4, Pallas kernels: 75.8 us -> 42.4 us  [the longest x1 34.2 us: run_core(): pl.pallas_call(core_kernel, grid=(classes,), in_specs=[pl.BlockSpec(featu...]
    all_to_all x1 -> x2, blocking collectives: 8.63 us -> 30.9 us  [the longest x1 22.1 us: per_device(): parts = lax.all_to_all(spread, 'depth', 0, 0, tiled=True)]
    ppermute x8 -> x4, waiting for transfers between devices: 9.85 us -> 27.7 us  [shift(): return lax.ppermute(value, axis, pairs)]
    all_to_all x1 -> x0, starting transfers between devices: 13 us -> none  [all_sum(): value = jnp.sum(lax.all_to_all(spread, axis, 0, 0, tiled=True), axis=0)]
    ppermute x8 -> x4, starting transfers between devices: 24.6 us -> 12.1 us  [shift(): return lax.ppermute(value, axis, pairs)]
    dot_general x3 -> x0, matrix products: 12.3 us -> none  [the longest x1 4.25 us: per_device(): jnp.einsum('kfdhw,cdhw->kfc', low, features, preferred_element_type=jnp.f...]
    all_to_all x1 -> x0, waiting for transfers between devices: 9.33 us -> none  [all_sum(): value = jnp.sum(lax.all_to_all(spread, axis, 0, 0, tiled=True), axis=0)]
    unnamed x40 -> x22, local copies, waits for them, and re-layouts: 2.25 us -> 7.09 us
  transfers between devices with their start and end apart: 9 -> 4, of which waited for: 5 -> 4; matrix products, arithmetic and copies ran while one was open for 2% -> 0% of each run, Pallas kernels for 0% -> 0%
where the time goes in v1:
time: 124 us; the launch traced here: 123 us
  Pallas kernels  42.4 us (34%)
  blocking collectives  30.9 us (25%)
  waiting for transfers between devices  27.7 us (22%)
  starting transfers between devices  12.1 us (10%)
  local copies, waits for them, and re-layouts  8.88 us (7%)
    pallas_call x1, Pallas kernels, run_core(): pl.pallas_call(core_kernel, grid=(classes,), in_specs=[pl.BlockSpec(featu...  34.2 us
    ppermute x4, waiting for transfers between devices, shift(): return lax.ppermute(value, axis, pairs)  27.7 us
    all_to_all x1, blocking collectives, per_device(): parts = lax.all_to_all(spread, 'depth', 0, 0, tiled=True)  22.1 us
    ppermute x4, starting transfers between devices, shift(): return lax.ppermute(value, axis, pairs)  12.1 us
    all_to_all x1, blocking collectives, per_device(): part = jnp.sum(lax.all_to_all(local, 'height', 0, 0, tiled=True), axis=0)  8.84 us
    unnamed x22, local copies, waits for them, and re-layouts  7.09 us
    pallas_call x1, Pallas kernels, run_tail(): pl.pallas_call(functools.partial(tail_kernel, cells), grid=(depth // step...  4.44 us
    pallas_call x1, Pallas kernels, run_head(): pl.pallas_call(head_kernel, grid=(depth,), in_specs=[pl.BlockSpec(memory_...  3.51 us
  transfers between devices with their start and end apart: 4, of which 4 were waited for; matrix products, arithmetic and copies ran while one was open for 0% of the time, Pallas kernels for 0%

profile of v1, /device:TPU:1, one launch (start us, length us, event | category | flops | bytes accessed | tf_op | source)
XLA Modules:
  0.0 123.5 jit_solution(2051091492735656791)
XLA Ops:
  0.6 0.7 convert_element_type.3.w_ref
  1.3 1.9 %copy-done = bf16[32,12,32,128]{3,2,1,0:T(8,128)(2,1)S(1)} copy-done((bf16[32,12,32,128]{3,2,1,0:T(8,128)(2,1)S(1)}, bf16[32,12,32,128]{3,2,1,0:T(8,128)(2,1)}, u32[]{:S(2)}) %copy-start) | copy-done | bytes 3145752
  3.2 1.1 copy-done.1
  4.3 0.7 copy-done.8
  4.9 3.5 %head.1 = (f32[3,12,32,128]{3,2,1,0:T(8,128)S(1)}, f32[3,12,32,128]{3,2,1,0:T(8,128)S(1)}, f32[3,480,128]{2,1,0:T(8,128)S(1)}, f32[3,480,128]{2,1,0:T(8,128)S(1)}) custom-call(f32[3,32]{1,0:T(4,128)S(1)} %convert_element_type.3.w_ref, f32[3]{0:T(128)S(1)} %copy-done.8, bf16[32,12,32,128]{3,2,1,0:T(8,128)(2,1)S(1)} %copy-done, s32[3,12,32,128]{3,2,1,0:T(8,128)S(1)} %copy-done.1), custom_call_target="tpu_custom_call" | custom-call | tf_op jit(solution)/shard_map/head/pallas_call | solution.py:81
  8.5 0.8 copy-done.7
  9.3 4.1 %collective-permute-start = (f32[3,480,128]{2,1,0:T(8,128)S(1)}, f32[3,480,128]{2,1,0:T(8,128)S(1)}, u32[]{:S(2)}, u32[]{:S(2)}) collective-permute-start(f32[3,480,128]{2,1,0:T(8,128)S(1)} %get-tuple-element.15), channel_id=1, source_target_pairs={{0,8},{8,16},{16,24},{24,32},{32,40},{40,48},{48,56},{56,64},{64,7... | collective-permute-start | bytes 2211848 | tf_op jit(solution)/shard_map/ppermute | solution.py:29
  13.3 1.3 %collective-permute-start.1 = (f32[3,480,128]{2,1,0:T(8,128)S(1)}, f32[3,480,128]{2,1,0:T(8,128)S(1)}, u32[]{:S(2)}, u32[]{:S(2)}) collective-permute-start(f32[3,480,128]{2,1,0:T(8,128)S(1)} %get-tuple-element.16), channel_id=1, source_target_pairs={{8,0},{16,8},{24,16},{32,24},{40,32},{48,40},{56,48},{64,56},{72,6... | collective-permute-start | bytes 2211848 | tf_op jit(solution)/shard_map/ppermute | solution.py:29
  14.6 13.8 %collective-permute-done.lo_ref.e_lo = f32[3,480,128]{2,1,0:T(8,128)S(1)} collective-permute-done((f32[3,480,128]{2,1,0:T(8,128)S(1)}, f32[3,480,128]{2,1,0:T(8,128)S(1)}, u32[]{:S(2)}, u32[]{:S(2)}) %collective-permute-start) | collective-permute-done | bytes 737312 | tf_op jit(solution)/shard_map/ppermute | solution.py:29
  28.4 3.8 %collective-permute-done.1.hi_ref.e_hi = f32[3,480,128]{2,1,0:T(8,128)S(1)} collective-permute-done((f32[3,480,128]{2,1,0:T(8,128)S(1)}, f32[3,480,128]{2,1,0:T(8,128)S(1)}, u32[]{:S(2)}, u32[]{:S(2)}) %collective-permute-start.1) | collective-permute-done | bytes 737312 | tf_op jit(solution)/shard_map/ppermute | solution.py:29
  32.3 0.2 side.1
  32.5 4.9 %collective-permute-start.2 = (f32[3,430,128]{2,1,0:T(8,128)S(1)}, f32[3,430,128]{2,1,0:T(8,128)S(1)}, u32[]{:S(2)}, u32[]{:S(2)}) collective-permute-start(f32[3,430,128]{2,1,0:T(8,128)S(1)} %get-tuple-element.17), channel_id=1, source_target_pairs={{0,1},{1,2},{2,3},{3,4},{4,5},{5,6},{6,7},{8,9},{9,10},{10,11},{11... | collective-permute-start | bytes 1981448 | tf_op jit(solution)/shard_map/ppermute | solution.py:29
  37.4 1.9 %collective-permute-start.3 = (f32[3,430,128]{2,1,0:T(8,128)S(1)}, f32[3,430,128]{2,1,0:T(8,128)S(1)}, u32[]{:S(2)}, u32[]{:S(2)}) collective-permute-start(f32[3,430,128]{2,1,0:T(8,128)S(1)} %get-tuple-element.18), channel_id=1, source_target_pairs={{1,0},{2,1},{3,2},{4,3},{5,4},{6,5},{7,6},{9,8},{10,9},{11,10},{12... | collective-permute-start | bytes 1981448 | tf_op jit(solution)/shard_map/ppermute | solution.py:29
  39.3 5.7 %collective-permute-done.2.e_left = f32[3,430,128]{2,1,0:T(8,128)S(1)} collective-permute-done((f32[3,430,128]{2,1,0:T(8,128)S(1)}, f32[3,430,128]{2,1,0:T(8,128)S(1)}, u32[]{:S(2)}, u32[]{:S(2)}) %collective-permute-start.2) | collective-permute-done | bytes 660512 | tf_op jit(solution)/shard_map/ppermute | solution.py:29
  45.0 4.4 %collective-permute-done.3.e_right = f32[3,430,128]{2,1,0:T(8,128)S(1)} collective-permute-done((f32[3,430,128]{2,1,0:T(8,128)S(1)}, f32[3,430,128]{2,1,0:T(8,128)S(1)}, u32[]{:S(2)}, u32[]{:S(2)}) %collective-permute-start.3) | collective-permute-done | bytes 660512 | tf_op jit(solution)/shard_map/ppermute | solution.py:29
  49.4 0.8 copy-done.10
  50.2 34.2 %core.1 = (f32[3,5,12,32,128]{4,3,2,1,0:T(8,128)}, f32[8,8,128]{2,1,0:T(8,128)}) custom-call(bf16[32,12,32,128]{3,2,1,0:T(8,128)(2,1)} %f_ref.3, f32[3,12,32,128]{3,2,1,0:T(8,128)} %copy-done.6, f32[3,480,128]{2,1,0:T(8,128)} %copy-done.4, f32[3,480,128]{2,1,0:T(8,128)} %copy-done.5, f32[3,430,128]{2,1,0:T(8,128)} %copy-done.9, f32[3,430,128]{2,1,0:T(8,128)} %copy-done.10, ...), custom_call_target="tpu_custom_call" | custom-call | tf_op jit(solution)/shard_map/core/pallas_call | solution.py:414
  84.4 8.8 %all_to_all.10 = f32[8,8,128]{2,1,0:T(8,128)S(1)} all-to-all(f32[8,8,128]{2,1,0:T(8,128)} %get-tuple-element.20), channel_id=1, replica_groups=mesh['depth'=32,'height'=8] {'height'}, dimensions={0} | all-to-all | bytes 65536 | tf_op jit(solution)/shard_map/all_to_all | solution.py:542
  93.3 22.1 %all_to_all.11.s_ref = f32[32,8,128]{2,1,0:T(8,128)S(1)} all-to-all(f32[32,8,128]{2,1,0:T(8,128)S(1)} %broadcast_in_dim.2), channel_id=1, replica_groups=mesh['depth'=32,'height'=8] {'depth'}, dimensions={0} | all-to-all | bytes 262144 | tf_op jit(solution)/shard_map/all_to_all | solution.py:544
  115.4 1.8 %copy-done.3 = f32[3,5,12,32,128]{4,3,2,1,0:T(8,128)S(1)} copy-done((f32[3,5,12,32,128]{4,3,2,1,0:T(8,128)S(1)}, f32[3,5,12,32,128]{4,3,2,1,0:T(8,128)}, u32[]{:S(2)}) %copy-start.3) | copy-done | bytes 2949144
  117.2 4.4 %tail.1 = (bf16[32,12,32,128]{3,2,1,0:T(8,128)(2,1)}, f32[8,128]{1,0:T(8,128)S(1)}) custom-call(f32[3,32]{1,0:T(4,128)S(1)} %convert_element_type.3.w_ref, f32[32,8,128]{2,1,0:T(8,128)S(1)} %all_to_all.11.s_ref, f32[3,5,12,32,128]{4,3,2,1,0:T(8,128)S(1)} %copy-done.3), custom_call_target="tpu_custom_call" | custom-call | tf_op jit(solution)/shard_map/tail/pallas_call | solution.py:508
  121.7 0.5 slice.9
  122.2 0.6 slice_bitcast_fusion
  122.8 0.7 reshape_squeeze.3
  (19 shorter events, 0.1 us)
Async XLA Ops:
  1.3 1.9 %copy-start = (bf16[32,12,32,128]{3,2,1,0:T(8,128)(2,1)S(1)}, bf16[32,12,32,128]{3,2,1,0:T(8,128)(2,1)}, u32[]{:S(2)}) copy-start(bf16[32,12,32,128]{3,2,1,0:T(8,128)(2,1)} %f_ref.3) | copy-start | bytes 9437188
  3.2 1.1 copy-start.1
  4.3 0.7 copy-start.8
  4.9 27.4 %copy-start.2 = (s32[3,12,32,128]{3,2,1,0:T(8,128)S(1)}, s32[3,12,32,128]{3,2,1,0:T(8,128)}, u32[]{:S(2)}) copy-start(s32[3,12,32,128]{3,2,1,0:T(8,128)} %l_own.1) | copy-start | bytes 1769476
  8.4 0.8 copy-start.7
  9.3 40.1 %copy-start.6 = (f32[3,12,32,128]{3,2,1,0:T(8,128)}, f32[3,12,32,128]{3,2,1,0:T(8,128)S(1)}, u32[]{:S(2)}) copy-start(f32[3,12,32,128]{3,2,1,0:T(8,128)S(1)} %get-tuple-element.14.e_ref.e_own) | copy-start | bytes 1769476
  9.3 19.2 %collective-permute-start = (f32[3,480,128]{2,1,0:T(8,128)S(1)}, f32[3,480,128]{2,1,0:T(8,128)S(1)}, u32[]{:S(2)}, u32[]{:S(2)}) collective-permute-start(f32[3,480,128]{2,1,0:T(8,128)S(1)} %get-tuple-element.15), channel_id=1, source_target_pairs={{0,8},{8,16},{16,24},{24,32},{32,40},{40,48},{48,56},{56,64},{64,7... | collective-permute-start | bytes 2211848 | tf_op jit(solution)/shard_map/ppermute | solution.py:29
  13.3 18.9 %collective-permute-start.1 = (f32[3,480,128]{2,1,0:T(8,128)S(1)}, f32[3,480,128]{2,1,0:T(8,128)S(1)}, u32[]{:S(2)}, u32[]{:S(2)}) collective-permute-start(f32[3,480,128]{2,1,0:T(8,128)S(1)} %get-tuple-element.16), channel_id=1, source_target_pairs={{8,0},{16,8},{24,16},{32,24},{40,32},{48,40},{56,48},{64,56},{72,6... | collective-permute-start | bytes 2211848 | tf_op jit(solution)/shard_map/ppermute | solution.py:29
  28.4 20.9 %copy-start.4 = (f32[3,480,128]{2,1,0:T(8,128)}, f32[3,480,128]{2,1,0:T(8,128)S(1)}, u32[]{:S(2)}) copy-start(f32[3,480,128]{2,1,0:T(8,128)S(1)} %collective-permute-done.lo_ref.e_lo) | copy-start | bytes 2211844
  32.3 17.1 %copy-start.5 = (f32[3,480,128]{2,1,0:T(8,128)}, f32[3,480,128]{2,1,0:T(8,128)S(1)}, u32[]{:S(2)}) copy-start(f32[3,480,128]{2,1,0:T(8,128)S(1)} %collective-permute-done.1.hi_ref.e_hi) | copy-start | bytes 2211844
  32.5 12.5 %collective-permute-start.2 = (f32[3,430,128]{2,1,0:T(8,128)S(1)}, f32[3,430,128]{2,1,0:T(8,128)S(1)}, u32[]{:S(2)}, u32[]{:S(2)}) collective-permute-start(f32[3,430,128]{2,1,0:T(8,128)S(1)} %get-tuple-element.17), channel_id=1, source_target_pairs={{0,1},{1,2},{2,3},{3,4},{4,5},{5,6},{6,7},{8,9},{9,10},{10,11},{11... | collective-permute-start | bytes 1981448 | tf_op jit(solution)/shard_map/ppermute | solution.py:29
  37.4 12.0 %collective-permute-start.3 = (f32[3,430,128]{2,1,0:T(8,128)S(1)}, f32[3,430,128]{2,1,0:T(8,128)S(1)}, u32[]{:S(2)}, u32[]{:S(2)}) collective-permute-start(f32[3,430,128]{2,1,0:T(8,128)S(1)} %get-tuple-element.18), channel_id=1, source_target_pairs={{1,0},{2,1},{3,2},{4,3},{5,4},{6,5},{7,6},{9,8},{10,9},{11,10},{12... | collective-permute-start | bytes 1981448 | tf_op jit(solution)/shard_map/ppermute | solution.py:29
  45.0 4.4 %copy-start.9 = (f32[3,430,128]{2,1,0:T(8,128)}, f32[3,430,128]{2,1,0:T(8,128)S(1)}, u32[]{:S(2)}) copy-start(f32[3,430,128]{2,1,0:T(8,128)S(1)} %collective-permute-done.2.e_left) | copy-start | bytes 1981444
  49.4 0.8 copy-start.10
  115.4 1.8 %copy-start.3 = (f32[3,5,12,32,128]{4,3,2,1,0:T(8,128)S(1)}, f32[3,5,12,32,128]{4,3,2,1,0:T(8,128)}, u32[]{:S(2)}) copy-start(f32[3,5,12,32,128]{4,3,2,1,0:T(8,128)} %get-tuple-element.21.x_ref) | copy-start | bytes 8847364

commit v2 on v1

v2 whole, which is shorter than its diff:
```python
import functools

import jax
import jax.numpy as jnp
from jax import lax
from jax.experimental import pallas as pl
from jax.experimental.pallas import tpu as pltpu
from jax.sharding import PartitionSpec as P

ITERS = 3
TAU = 0.1
SHARP = 0.05
ALPHA = 0.3
BETA = 0.7
HALO = 10
LHALO = 5
ROWS = 80
OFF = 24
NB = 4
MXU = 4
CHUNK = 4
FIELDS = 5
EARLY = 3
EXACT = lax.Precision.HIGHEST
LAST = (((1,), (1,)), ((), ()))


def shift(value, axis, step):
    n = lax.axis_size(axis)
    pairs = [(i, i + step) for i in range(n) if 0 <= i + step < n]
    return lax.ppermute(value, axis, pairs)


def head_kernel(w_hbm, b_hbm, f_hbm, l_hbm, p_ref, e_ref, first_ref, last_ref, spread_ref, F, L, W, B, sems):
    channels, depth, height, wd = F.shape
    classes = p_ref.shape[0]
    small = [
        pltpu.make_async_copy(w_hbm, W, sems.at[depth]),
        pltpu.make_async_copy(b_hbm, B, sems.at[depth + 1]),
    ]
    edges = [
        pltpu.make_async_copy(l_hbm.at[:, 0:LHALO], L.at[0], sems.at[depth + 2]),
        pltpu.make_async_copy(l_hbm.at[:, depth - LHALO : depth], L.at[1], sems.at[depth + 3]),
    ]
    planes = [
        pltpu.make_async_copy(f_hbm.at[:, d], F.at[:, d], sems.at[d]) for d in range(depth)
    ]
    for copy in small + planes + edges:
        copy.start()
    for copy in small:
        copy.wait()
    weight = W[...].astype(jnp.float32)
    for k in range(classes):
        for c in range(channels):
            spread_ref[k, c : c + 1, :] = jnp.broadcast_to(weight[k : k + 1, c : c + 1], (1, wd))
    bias = [jnp.broadcast_to(B[0:1, k : k + 1], (height, wd)) for k in range(classes)]
    for d in range(depth):
        planes[d].wait()
        acc = [None] * classes
        for c in range(channels):
            f = F[c, d].astype(jnp.float32)
            for k in range(classes):
                term = jnp.broadcast_to(spread_ref[k, c : c + 1, :], (height, wd)) * f
                acc[k] = term if c == 0 else acc[k] + term
        for k in range(classes):
            prob = 1.0 / (1.0 + jnp.exp(-(acc[k] + bias[k])))
            p_ref[k, d] = prob
            e = jnp.exp(prob * (-1.0 / TAU))
            e_ref[k, d] = e
            if d < HALO:
                first_ref[k, d * height : (d + 1) * height, :] = e
            if d >= depth - HALO:
                at = (d - (depth - HALO)) * height
                last_ref[k, at : at + height, :] = e
    for copy, n, out in zip(edges, range(2), (first_ref, last_ref)):
        copy.wait()
        for k in range(classes):
            for p in range(LHALO):
                at = (HALO + p) * height
                out[k, at : at + height, :] = L[n, k, p].astype(jnp.float32)


VMEM = pl.BlockSpec(memory_space=pltpu.VMEM)
HBM = pl.BlockSpec(memory_space=pltpu.HBM)


def run_head(weight, bias, features, labels):
    classes, channels = weight.shape
    depth, height, wd = features.shape[1:]
    full = jax.ShapeDtypeStruct((classes, depth, height, wd), jnp.float32)
    edge = jax.ShapeDtypeStruct((classes, (HALO + LHALO) * height, wd), jnp.float32)
    return pl.pallas_call(
        head_kernel,
        in_specs=[HBM] * 4,
        out_specs=[VMEM] * 5,
        out_shape=[full, full, edge, edge, jax.ShapeDtypeStruct((classes, channels, wd), jnp.float32)],
        scratch_shapes=[
            pltpu.VMEM(features.shape, features.dtype),
            pltpu.VMEM((2, classes, LHALO, height, wd), jnp.int32),
            pltpu.VMEM(weight.shape, weight.dtype),
            pltpu.VMEM((1, classes), jnp.float32),
            pltpu.SemaphoreType.DMA((depth + 4,)),
        ],
        compiler_params=pltpu.CompilerParams(vmem_limit_bytes=62 * 2**20),
        name="head",
    )(weight, bias.reshape(1, classes), features, labels)


def side_kernel(own_ref, lab_ref, lo_ref, hi_ref, first_ref, last_ref):
    classes, depth, height = own_ref.shape[:3]
    for k in range(classes):
        for out, near in ((first_ref, True), (last_ref, False)):
            base, skip = 0, 0
            for ref, width in ((own_ref, HALO), (lab_ref, LHALO)):
                at = 0 if near else height - width
                for p in range(depth + 2 * width):
                    if p < width:
                        v = lo_ref[k, pl.ds((skip + p) * height + at, width), :]
                    elif p < width + depth:
                        v = ref[k, p - width, pl.ds(at, width), :].astype(jnp.float32)
                    else:
                        v = hi_ref[k, pl.ds((skip + p - width - depth) * height + at, width), :]
                    out[k, pl.ds(base + p * width, width), :] = v
                base += width * (depth + 2 * width)
                skip += width


def run_side(own, labels, lo, hi):
    classes, depth, height, wd = own.shape
    rows = HALO * (depth + 2 * HALO) + LHALO * (depth + 2 * LHALO)
    edge = jax.ShapeDtypeStruct((classes, rows, wd), jnp.float32)
    return pl.pallas_call(
        side_kernel,
        in_specs=[VMEM] * 4,
        out_specs=[VMEM] * 2,
        out_shape=[edge, edge],
        compiler_params=pltpu.CompilerParams(vmem_limit_bytes=16 * 2**20),
        name="side",
    )(own, labels, lo, hi)


def stash(S, group, plane, value):
    height, wd = value.shape
    high = value.astype(jnp.bfloat16)
    low = (value - high.astype(jnp.float32)).astype(jnp.bfloat16)
    for t in range(height // 16):
        at = (plane * (height // 16) + t) * wd
        S[32 * group : 32 * group + 16, at : at + wd] = high[16 * t : 16 * t + 16]
        S[32 * group + 16 : 32 * group + 32, at : at + wd] = low[16 * t : 16 * t + 16]


def contract(f_ref, S):
    channels, depth, height, wd = f_ref.shape
    cols = S.shape[0]
    total = None
    for d in range(0, depth, CHUNK):
        f = jnp.concatenate(
            [
                f_ref[:, d + i, 16 * t : 16 * t + 16, :].reshape(channels * 16, wd)
                for i in range(CHUNK)
                for t in range(height // 16)
            ],
            axis=1,
        )
        n = height // 16 * wd
        got = lax.dot_general(f, S[:, d * n : (d + CHUNK) * n], LAST, preferred_element_type=jnp.float32)
        total = got if total is None else total + got
    h = lax.broadcasted_iota(jnp.int32, (channels, 16, cols), 1)
    g = lax.broadcasted_iota(jnp.int32, (channels, 16, cols), 2) % 16
    return jnp.sum(jnp.where(h == g, total.reshape(channels, 16, cols), 0.0), axis=1)


def collect(m, fields):
    cols = m.shape[1]
    item = lax.broadcasted_iota(jnp.int32, (8, cols), 0)
    at = lax.broadcasted_iota(jnp.int32, (8, cols), 1) // 32
    pick = jnp.zeros((8, cols), jnp.float32)
    for row, group in enumerate(fields):
        if group is not None:
            pick = jnp.where((item == row) & (at == group), 1.0, pick)
    return lax.dot_general(pick, m, LAST, precision=EXACT)


def by_rows(values, lane):
    wd = next(v for v in values if v is not None).shape[1]
    values = [jnp.zeros((1, wd), jnp.float32) if v is None else jnp.sum(v, axis=0, keepdims=True) for v in values]
    values += [jnp.zeros((1, wd), jnp.float32)] * (8 - len(values))
    col = lax.broadcasted_iota(jnp.int32, (wd, wd // 4), 1)
    return jnp.dot(jnp.concatenate(values, axis=0), jnp.where(col == lane, 1.0, 0.0), precision=EXACT)


def early_kernel(f_ref, l_ref, p_ref, k_ref, sum_ref, S):
    classes, depth, height, wd = p_ref.shape
    parts = None
    for k in range(classes):
        sums = [None] * 8
        for d in range(depth):
            prob = p_ref[k, d]
            lab = l_ref[k, d].astype(jnp.float32)
            lsk = k_ref[k, d].astype(jnp.float32)
            slope = prob * (1.0 - prob)
            fields = [slope * lab, slope, slope * lsk]
            for n, v in enumerate([prob * lab, prob, lab, lsk * prob, lsk] + fields):
                sums[n] = v if sums[n] is None else sums[n] + v
            for f, v in enumerate(fields):
                stash(S, k * EARLY + f, d, v)
        here = by_rows(sums[:3] + [None, None] + sums[3:5], k) + by_rows(sums[5:], classes + k)
        parts = here if parts is None else parts + here
    m = contract(f_ref, S)
    heads = [collect(m, [k * EARLY + f for f in range(EARLY)]) for k in range(classes)]
    sum_ref[...] = jnp.concatenate(heads + [parts], axis=1)


def run_early(features, labels, prob, lsk):
    classes, depth, height, wd = prob.shape
    return pl.pallas_call(
        early_kernel,
        in_specs=[VMEM] * 4,
        out_specs=VMEM,
        out_shape=jax.ShapeDtypeStruct((8, wd), jnp.float32),
        scratch_shapes=[pltpu.VMEM((classes * EARLY * 32, depth * (height // 16) * wd), jnp.bfloat16)],
        compiler_params=pltpu.CompilerParams(vmem_limit_bytes=24 * 2**20),
        cost_estimate=pl.CostEstimate(flops=10**9, bytes_accessed=10**7, transcendentals=0),
        name="early",
    )(features, labels, prob, lsk)


def wide_sums(values, lane, band):
    rows, width = values[0].shape
    out = []
    if MXU:
        s = jnp.concatenate(values[:MXU], axis=0)
        high = s.astype(jnp.bfloat16)
        low = (s - high.astype(jnp.float32)).astype(jnp.bfloat16)
        s = jnp.dot(jnp.concatenate([high, low], axis=1), band, preferred_element_type=jnp.float32)
        out = [s[i * rows : (i + 1) * rows] for i in range(MXU)]
    for s in values[MXU:]:
        left = jnp.where(lane == 0, 0.0, pltpu.roll(s, 1, 1))
        right = jnp.where(lane == width - 1, 0.0, pltpu.roll(s, width - 1, 1))
        out.append(s + left + right)
    return out


def boxes(load, d, r0, nr, lane, band):
    h = []
    for i in range(NB + 2):
        h.append(load(d + i - 1, r0 - 1, nr) + load(d + i - 1, r0, nr) + load(d + i - 1, r0 + 1, nr))
    out = []
    for i in range(0, NB, 2):
        mid = h[i + 1] + h[i + 2]
        out.append(h[i] + mid)
        out.append(mid + h[i + 3])
    return wide_sums(out, lane, band)


def sweep(first, last, body):
    for i in range(first, last, NB):
        body(min(i, last - NB))


def core_kernel(
    k, classes,
    before_ref, f_ref, e_own, lo, hi, left, right, l_own, p_own, k_own,
    x_ref, sum_ref,
    E, R, X, U, V, Q, L, S,
):
    depth, height, wd = p_own.shape[1:]
    planes = depth + 2 * HALO
    lplanes = depth + 2 * LHALO
    base = HALO - LHALO

    row = lax.broadcasted_iota(jnp.int32, (2 * wd, wd), 0)
    col = lax.broadcasted_iota(jnp.int32, (2 * wd, wd), 1)
    near = jnp.abs(jnp.where(row < wd, row, row - wd) - col) <= 1
    band = jnp.where(near, 1.0, 0.0).astype(jnp.bfloat16)

    E[0, :, OFF - HALO - 8 : OFF - HALO, :] = jnp.zeros((planes, 8, wd), jnp.float32)
    E[0, :, OFF + height + HALO : OFF + height + HALO + 8, :] = jnp.zeros((planes, 8, wd), jnp.float32)
    L[:, OFF - 8 : OFF - LHALO, :] = jnp.zeros((lplanes, 8 - LHALO, wd), jnp.float32)
    L[:, OFF + height + LHALO : OFF + height + 8, :] = jnp.zeros((lplanes, 8 - LHALO, wd), jnp.float32)

    def gather(put, width, own, skip, base):
        put(slice(width, width + depth), slice(OFF, OFF + height), own[k])
        for p in range(width):
            rows = slice((skip + p) * height, (skip + p + 1) * height)
            put(p, slice(OFF, OFF + height), lo[k, rows, :])
            put(width + depth + p, slice(OFF, OFF + height), hi[k, rows, :])
        for p in range(depth + 2 * width):
            rows = slice(base + p * width, base + (p + 1) * width)
            put(p, slice(OFF - width, OFF), left[k, rows, :])
            put(p, slice(OFF + height, OFF + height + width), right[k, rows, :])

    def put_e(p, rows, v):
        E[0, p, rows, :] = v

    def put_l(p, rows, v):
        L[p, rows, :] = v.astype(jnp.float32)

    gather(put_e, HALO, e_own, 0, 0)
    gather(put_l, LHALO, l_own, HALO, HALO * planes)
    w0, wn = OFF - 8, height + 16
    lane = lax.broadcasted_iota(jnp.int32, (wn, wd), 1)
    lane_big = lax.broadcasted_iota(jnp.int32, (wn + 16, wd), 1)
    lane_own = lax.broadcasted_iota(jnp.int32, (height, wd), 1)

    for j in range(ITERS + 1):
        r0, nr, ln = (w0 - 8, wn + 16, lane_big) if j == 0 else (w0, wn, lane)

        def erode(d, j=j, r0=r0, nr=nr, ln=ln):
            outs = boxes(lambda a, b, n: E[j, a, pl.ds(b, n), :], d, r0, nr, ln, band)
            for i, s in enumerate(outs):
                live = E[0, d + i, pl.ds(r0, nr), :] > 0.0
                E[j + 1, d + i, pl.ds(r0, nr), :] = jnp.where(live, s, 0.0)
                R[j, d + i, pl.ds(r0, nr), :] = jnp.where(live, 1.0 / s, 0.0)

        sweep(j + 1, planes - j - 1, erode)

    for j in range(ITERS + 1):

        def dilate(d, j=j):
            outs = boxes(lambda a, b, n: R[j, a, pl.ds(b, n), :], d, w0, wn, lane, band)
            for i, s in enumerate(outs):
                live = E[0, d + i, pl.ds(w0, wn), :] > 0.0
                rd = 1.0 / s
                t = rd * R[j - 1, d + i, pl.ds(w0, wn), :] if j else rd / E[0, d + i, pl.ds(w0, wn), :]
                U[j, d + i - base, pl.ds(w0, wn), :] = jnp.where(live, rd, 0.0)
                X[j, d + i - base, pl.ds(w0, wn), :] = jnp.where(live, t * t, 0.0)

        sweep(base, planes - base, dilate)

    row = lax.broadcasted_iota(jnp.int32, (wn, wd), 0)
    inner = jnp.where((row >= OFF - w0) & (row < OFF - w0 + height), 1.0, 0.0)

    def point(d, carry):
        rows = pl.ds(w0, wn)
        x = [X[j, d, rows, :] for j in range(ITERS + 1)]
        opx = [1.0 + v for v in x]
        logs = [jnp.log(v) for v in opx]
        skel = SHARP * logs[0]
        om, e, ope = [None], [None], [None]
        for j in range(1, ITERS + 1):
            om.append(1.0 - skel)
            e.append(jnp.exp(logs[j] * om[j]))
            ope.append(1.0 + e[j])
            skel = skel + SHARP * jnp.log(ope[j])
        lab = L[d, rows, :]
        g = None
        for j in range(ITERS, -1, -1):
            if j:
                both = 1.0 / (opx[j] * ope[j])
                gv = x[j] * e[j] * om[j] * both
                keep = 1.0 - (SHARP * logs[j]) * (e[j] * opx[j] * both)
            else:
                gv = x[0] / opx[0]
            if g is not None:
                gv = gv * g
            if j:
                g = keep if g is None else g * keep
            u = gv * U[j, d, rows, :]
            X[j, d, rows, :] = gv
            U[j, d, rows, :] = u
            V[j, d, rows, :] = u * lab
        own = jnp.where((d >= LHALO) & (d < LHALO + depth), 1.0, 0.0)
        skel = skel * (inner * own)
        return carry[0] + skel * lab, carry[1] + skel

    zero = jnp.zeros((wn, wd), jnp.float32)
    sky, sk = lax.fori_loop(0, lplanes, point, (zero, zero), unroll=2)

    for j in range(ITERS + 1, 0, -1):
        now, nxt = j % 2, (j + 1) % 2

        def back(d, j=j, now=now, nxt=nxt):
            b = d - base
            for which, src in ((0, V), (1, U)):
                du = boxes(lambda a, c, n: src[j - 1, a, pl.ds(c, n), :], b, w0, wn, lane, band)
                if j <= ITERS:
                    dq = boxes(lambda a, c, n: Q[which, nxt, a, pl.ds(c, n), :], b, w0, wn, lane, band)
                for i in range(NB):
                    r = R[j - 1, d + i, pl.ds(w0, wn), :]
                    v = -r * du[i]
                    if j <= ITERS:
                        live = E[0, d + i, pl.ds(w0, wn), :] > 0.0
                        gv = X[j, b + i, pl.ds(w0, wn), :]
                        if which == 0:
                            gv = gv * L[b + i, pl.ds(w0, wn), :]
                        v = jnp.where(live, r * (gv + v) + dq[i], 0.0)
                    else:
                        v = r * v
                    Q[which, now, b + i, pl.ds(w0, wn), :] = v

        sweep(HALO - j, planes - HALO + j, back)

    sums = [jnp.zeros((height, wd), jnp.float32) for _ in range(FIELDS - EARLY)]

    def last(d):
        b = d - base
        o = d - HALO
        grads = [
            boxes(lambda a, c, n: Q[which, 1, a, pl.ds(c, n), :], b, OFF, height, lane_own, band)
            for which in range(2)
        ]
        for i in range(NB):
            e = E[0, d + i, pl.ds(OFF, height), :]
            gv = X[0, b + i, pl.ds(OFF, height), :]
            prob = p_own[k, o + i]
            lab = L[b + i, pl.ds(OFF, height), :]
            slope = prob * (1.0 - prob)
            fields = [slope * (gv * lab + e * grads[0][i]), slope * (gv + e * grads[1][i])]
            for f, v in enumerate(fields):
                sums[f] = sums[f] + v
                x_ref[2 + f, o + i] = v
                stash(S, f, o + i, v)
            x_ref[0, o + i] = slope
            x_ref[1, o + i] = lab + 2.0 * k_own[k, o + i].astype(jnp.float32)

    sweep(HALO, HALO + depth, last)
    parts = by_rows([None] * 3 + [sky, sk], k) + by_rows([None] * EARLY + sums, classes + k)
    heads = collect(contract(f_ref, S), [None] * EARLY + [0, 1])
    blank = jnp.zeros_like(heads)
    whole = jnp.concatenate([heads if n == k else blank for n in range(classes)] + [parts], axis=1)
    whole = whole + before_ref[...]
    for n in range(sum_ref.shape[0]):
        sum_ref[n] = whole


def run_core(k, copies, before, features, own, near, labels, prob, lsk):
    classes, depth, height, wd = prob.shape
    planes = depth + 2 * HALO
    lplanes = depth + 2 * LHALO
    args = (before, features, own, *near, labels, prob, lsk)
    n = ITERS + 1
    fields = jax.ShapeDtypeStruct((4, depth, height, wd), jnp.float32)
    sums = jax.ShapeDtypeStruct((copies, 8, wd), jnp.float32)
    return pl.pallas_call(
        functools.partial(core_kernel, k, classes),
        in_specs=[VMEM] * len(args),
        out_specs=[VMEM] * 2,
        out_shape=[fields, sums],
        scratch_shapes=[
            pltpu.VMEM((n + 1, planes, ROWS, wd), jnp.float32),
            pltpu.VMEM((n, planes, ROWS, wd), jnp.float32),
            pltpu.VMEM((n, lplanes, ROWS, wd), jnp.float32),
            pltpu.VMEM((n, lplanes, ROWS, wd), jnp.float32),
            pltpu.VMEM((n, lplanes, ROWS, wd), jnp.float32),
            pltpu.VMEM((2, 2, lplanes, ROWS, wd), jnp.float32),
            pltpu.VMEM((lplanes, ROWS, wd), jnp.float32),
            pltpu.VMEM(((FIELDS - EARLY) * 32, depth * (height // 16) * wd), jnp.bfloat16),
        ],
        compiler_params=pltpu.CompilerParams(vmem_limit_bytes=34 * 2**20),
        cost_estimate=pl.CostEstimate(flops=2 * 10**10, bytes_accessed=4 * 10**7, transcendentals=0),
        name=f"core{k}",
    )(*args)


def tail_kernel(cells, w_ref, s_ref, *refs):
    classes = len(refs) - 5
    x_ref = refs[:classes]
    g_ref, loss_ref, gw_ref, gb_ref, C = refs[classes:]
    channels = g_ref.shape[0]
    quarter = s_ref.shape[2] // 4
    wd = s_ref.shape[2]

    @pl.when(pl.program_id(0) == 0)
    def _():
        total = jnp.sum(s_ref[...], axis=0)
        tp, sp, sl, sky, sk, lsp, ls = [jnp.broadcast_to(total[i : i + 1], total.shape) for i in range(7)]
        prec = (sky + 1.0) / (sk + 1.0)
        sens = (lsp + 1.0) / (ls + 1.0)
        both = prec + sens
        cldice = 1.0 - 2.0 * prec * sens / both
        bottom = tp + ALPHA * (sp - tp) + BETA * (sl - tp) + 1.0
        tversky = (tp + 1.0) / bottom
        term = cldice + 1.0 - tversky
        scale = cells / classes
        by_prec = -2.0 * (sens / both) * (sens / both) * scale
        by_sens = -2.0 * (prec / both) * (prec / both) * scale
        by_sky = by_prec / (sk + 1.0)
        by_sk = -by_sky * prec
        by_lsp = by_sens / (ls + 1.0)
        by_sp = scale * ALPHA * tversky / bottom
        by_tp = scale * (tversky * (1.0 - ALPHA - BETA) - 1.0) / bottom
        lane = lax.broadcasted_iota(jnp.int32, total.shape, 1)
        item = lax.broadcasted_iota(jnp.int32, total.shape, 0)
        mult = jnp.zeros_like(total)
        loss = jnp.zeros_like(total)
        for k in range(classes):
            mine = (lane // quarter == k) | (lane == classes * (quarter + 1) + k)
            spot = lane == classes * quarter + k

            def pick(v):
                return jnp.sum(jnp.where(spot, v, 0.0), axis=1, keepdims=True)

            for f, v in enumerate((by_tp, by_sp, by_lsp, by_sky, by_sk)):
                v = jnp.broadcast_to(pick(v), total.shape)
                C[k, f] = v
                mult = jnp.where(mine & (item == f), v, mult)
            loss = loss + pick(term) * (1.0 / classes)
        grad = jnp.sum(jnp.where(item < FIELDS, total * mult, 0.0), axis=0, keepdims=True)
        square = jnp.sum(grad * grad, axis=1, keepdims=True)
        rms = jnp.sqrt(square / (classes * channels + classes) + 1e-06)
        grad = grad / rms
        loss_ref[...] = loss[0:1, 0:1]
        gw_ref[...] = jnp.concatenate([grad[:, k * quarter : (k + 1) * quarter] for k in range(classes)], axis=0)
        n = classes * (quarter + 1)
        gb_ref[...] = grad[:, n : n + classes]

    height = g_ref.shape[2]
    base = pl.program_id(0) * g_ref.shape[1]
    for p in range(g_ref.shape[1]):
        for t in range(height // 16):
            rows = slice(16 * t, 16 * t + 16)
            dlogit = []
            for k in range(classes):
                c = [jnp.concatenate([C[k, f]] * 2, axis=0) for f in range(FIELDS)]
                slope, code, ga, gb = [x_ref[k][f, base + p, rows, :] for f in range(4)]
                lsk = code >= 2.0
                lab = jnp.where(lsk, code - 2.0, code)
                v = slope * (c[0] * lab + c[1] + jnp.where(lsk, c[2], 0.0)) + c[3] * ga + c[4] * gb
                dlogit.append(v)
            for c in range(channels):
                v = None
                for k in range(classes):
                    term = jnp.broadcast_to(w_ref[k, c : c + 1, :], (16, wd)) * dlogit[k]
                    v = term if v is None else v + term
                g_ref[c, p, rows, :] = v.astype(jnp.bfloat16)


def run_tail(cells, spread, sums, fields):
    depth, height, wd = fields[0].shape[1:]
    classes, channels = spread.shape[:2]
    step = 2
    return pl.pallas_call(
        functools.partial(tail_kernel, cells),
        grid=(depth // step,),
        in_specs=[VMEM] * (2 + classes),
        out_specs=[
            pl.BlockSpec((channels, step, height, wd), lambda d: (0, d, 0, 0)),
            pl.BlockSpec((1, 1), lambda d: (0, 0)),
            pl.BlockSpec((classes, channels), lambda d: (0, 0)),
            pl.BlockSpec((1, classes), lambda d: (0, 0)),
        ],
        out_shape=[
            jax.ShapeDtypeStruct((channels, depth, height, wd), jnp.bfloat16),
            jax.ShapeDtypeStruct((1, 1), jnp.float32),
            jax.ShapeDtypeStruct((classes, channels), jnp.float32),
            jax.ShapeDtypeStruct((1, classes), jnp.float32),
        ],
        scratch_shapes=[pltpu.VMEM((classes, FIELDS, 8, wd), jnp.float32)],
        compiler_params=pltpu.CompilerParams(vmem_limit_bytes=16 * 2**20),
        name="tail",
    )(spread, sums, *fields)


def per_device(features, head_weight, head_bias, labels, label_skeleton):
    classes, channels = head_weight.shape
    _, block_d, block_h, wd = features.shape
    cells = block_d * lax.axis_size("depth") * block_h * lax.axis_size("height") * wd
    prob, own, first, last, spread = run_head(head_weight, head_bias, features, labels)
    lo, hi = shift(last, "depth", 1), shift(first, "depth", -1)
    local = run_early(features, labels, prob, label_skeleton)
    lo, hi, local = lax.optimization_barrier((lo, hi, local))
    first, last = run_side(own, labels, lo, hi)
    near = (lo, hi, shift(last, "height", 1), shift(first, "height", -1))
    fields = []
    for k in range(classes):
        copies = lax.axis_size("height") if k == classes - 1 else 1
        mine, local = run_core(k, copies, local, features, own, near, labels, prob, label_skeleton)
        fields.append(mine)
        if copies == 1:
            local = local[0]
    part = jnp.sum(lax.all_to_all(local, "height", 0, 0, tiled=True), axis=0)
    part = jnp.broadcast_to(part[None], (lax.axis_size("depth"),) + part.shape)
    parts = lax.all_to_all(part, "depth", 0, 0, tiled=True)
    grad_features, loss, grad_w, grad_b = run_tail(cells, spread, parts, fields)
    return loss[0, 0], grad_features, grad_w, grad_b[0]


def solution(mesh):
    return jax.shard_map(
        per_device,
        mesh=mesh,
        in_specs=(
            P(None, "depth", "height", None),
            P(),
            P(),
            P(None, "depth", "height", None),
            P(None, "depth", "height", None),
        ),
        out_specs=(P(), P(None, "depth", "height", None), P(), P()),
        check_vma=False,
    )
```

time: 124 us -> 108 us (0.87)
  waiting for transfers between devices: 27.7 us -> 21.8 us
  Pallas kernels: 42.4 us -> 37 us
  local copies, waits for them, and re-layouts: 8.88 us -> 5.03 us
    ppermute x4, waiting for transfers between devices: 27.7 us -> 21.8 us  [shift(): return lax.ppermute(value, axis, pairs)]
    pallas_call x3 -> x6, Pallas kernels: 37.9 us -> 33.3 us  [the longest x3 25.4 us: run_core(): pl.pallas_call(functools.partial(core_kernel, k, classes), in_specs=[VMEM...]
    unnamed x22 -> x20, local copies, waits for them, and re-layouts: 7.09 us -> 5.01 us
  transfers between devices with their start and end apart: 4 -> 4, of which waited for: 4 -> 4; matrix products, arithmetic and copies ran while one was open for 0% -> 0% of each run, Pallas kernels for 0% -> 3%
where the time goes in v2:
time: 108 us
  Pallas kernels  37 us (34%)
  blocking collectives  30.7 us (28%)
  waiting for transfers between devices  21.8 us (20%)
  starting transfers between devices  12.5 us (12%)
  local copies, waits for them, and re-layouts  5.03 us (5%)
    pallas_call x3, Pallas kernels, run_core(): pl.pallas_call(functools.partial(core_kernel, k, classes), in_specs=[VMEM...  25.4 us
    all_to_all x1, blocking collectives, per_device(): parts = lax.all_to_all(part, 'depth', 0, 0, tiled=True)  22.1 us
    ppermute x4, waiting for transfers between devices, shift(): return lax.ppermute(value, axis, pairs)  21.8 us
    ppermute x4, starting transfers between devices, shift(): return lax.ppermute(value, axis, pairs)  12.5 us
    all_to_all x1, blocking collectives, per_device(): part = jnp.sum(lax.all_to_all(local, 'height', 0, 0, tiled=True), axis=0)  8.62 us
    unnamed x20, local copies, waits for them, and re-layouts  5.01 us
    pallas_call x1, Pallas kernels, run_head(): pl.pallas_call(head_kernel, in_specs=[HBM] * 4, out_specs=[VMEM] * 5, out...  4.89 us
    pallas_call x1, Pallas kernels, run_tail(): pl.pallas_call(functools.partial(tail_kernel, cells), grid=(depth // step...  3.64 us
  transfers between devices with their start and end apart: 4, of which 4 were waited for; matrix products, arithmetic and copies ran while one was open for 0% of the time, Pallas kernels for 3%

profile of v2, /device:TPU:1, one launch (start us, length us, event | category | flops | bytes accessed | tf_op | source)
XLA Modules:
  0.0 107.8 jit_solution(12739912330633117312)
XLA Ops:
  0.6 0.0 copy-start.2
  0.6 0.0 copy-start.5
  0.7 4.9 %head.1 = (f32[3,12,32,128]{3,2,1,0:T(8,128)}, f32[3,12,32,128]{3,2,1,0:T(8,128)}, f32[3,480,128]{2,1,0:T(8,128)}, f32[3,480,128]{2,1,0:T(8,128)}, f32[3,32,128]{2,1,0:T(8,128)}) custom-call(bf16[3,32]{1,0:T(4,128)(2,1)} %w_hbm.1, f32[1,3]{1,0:T(1,128)} %bitcast.7, bf16[32,12,32,128]{3,2,1,0:T(8,128)(2,1)} %f_ref.7, s32[3,12,32,128]{3,2,1,0:T(8,128)} %l_own.5), custom_call_target="tpu_custom_call" | custom-call | tf_op jit(solution)/shard_map/head/pallas_call | solution.py:92
  5.5 4.1 %collective-permute-start = (f32[3,480,128]{2,1,0:T(8,128)}, f32[3,480,128]{2,1,0:T(8,128)S(1)}, u32[]{:S(2)}, u32[]{:S(2)}) collective-permute-start(f32[3,480,128]{2,1,0:T(8,128)} %get-tuple-element.25), channel_id=1, source_target_pairs={{0,8},{8,16},{16,24},{24,32},{32,40},{40,48},{48,56},{56,64},{64,7... | collective-permute-start | bytes 2211848 | tf_op jit(solution)/shard_map/ppermute | solution.py:31
  9.6 1.3 %collective-permute-start.1 = (f32[3,480,128]{2,1,0:T(8,128)}, f32[3,480,128]{2,1,0:T(8,128)S(1)}, u32[]{:S(2)}, u32[]{:S(2)}) collective-permute-start(f32[3,480,128]{2,1,0:T(8,128)} %get-tuple-element.26), channel_id=1, source_target_pairs={{8,0},{16,8},{24,16},{32,24},{40,32},{48,40},{56,48},{64,56},{72,6... | collective-permute-start | bytes 2211848 | tf_op jit(solution)/shard_map/ppermute | solution.py:31
  11.0 0.0 copy-start
  11.0 1.9 %copy-done = bf16[32,12,32,128]{3,2,1,0:T(8,128)(2,1)S(1)} copy-done((bf16[32,12,32,128]{3,2,1,0:T(8,128)(2,1)S(1)}, bf16[32,12,32,128]{3,2,1,0:T(8,128)(2,1)}, u32[]{:S(2)}) %copy-start) | copy-done | bytes 3145752
  12.8 1.1 copy-done.6
  13.9 2.9 %early.1.before_ref = f32[8,128]{1,0:T(8,128)S(1)} custom-call(bf16[32,12,32,128]{3,2,1,0:T(8,128)(2,1)S(1)} %copy-done, s32[3,12,32,128]{3,2,1,0:T(8,128)S(1)} %copy-done.2, f32[3,12,32,128]{3,2,1,0:T(8,128)S(1)} %copy-done.6, s32[3,12,32,128]{3,2,1,0:T(8,128)S(1)} %copy-done.5), custom_call_target="tpu_custom_call" | custom-call | flops 1000000000 | bytes 10000000 | tf_op jit(solution)/shard_map/early/pallas_call | solution.py:216
  16.8 8.2 %collective-permute-done.lo_ref.lo = f32[3,480,128]{2,1,0:T(8,128)S(1)} collective-permute-done((f32[3,480,128]{2,1,0:T(8,128)}, f32[3,480,128]{2,1,0:T(8,128)S(1)}, u32[]{:S(2)}, u32[]{:S(2)}) %collective-permute-start) | collective-permute-done | bytes 737312 | tf_op jit(solution)/shard_map/ppermute | solution.py:31
  25.0 3.7 %collective-permute-done.1.hi_ref.hi = f32[3,480,128]{2,1,0:T(8,128)S(1)} collective-permute-done((f32[3,480,128]{2,1,0:T(8,128)}, f32[3,480,128]{2,1,0:T(8,128)S(1)}, u32[]{:S(2)}, u32[]{:S(2)}) %collective-permute-start.1) | collective-permute-done | bytes 737312 | tf_op jit(solution)/shard_map/ppermute | solution.py:31
  28.8 0.2 side.1
  28.9 4.9 %collective-permute-start.2 = (f32[3,430,128]{2,1,0:T(8,128)S(1)}, f32[3,430,128]{2,1,0:T(8,128)S(1)}, u32[]{:S(2)}, u32[]{:S(2)}) collective-permute-start(f32[3,430,128]{2,1,0:T(8,128)S(1)} %get-tuple-element.32), channel_id=1, source_target_pairs={{0,1},{1,2},{2,3},{3,4},{4,5},{5,6},{6,7},{8,9},{9,10},{10,11},{11... | collective-permute-start | bytes 1981448 | tf_op jit(solution)/shard_map/ppermute | solution.py:31
  33.8 2.2 %collective-permute-start.3 = (f32[3,430,128]{2,1,0:T(8,128)S(1)}, f32[3,430,128]{2,1,0:T(8,128)S(1)}, u32[]{:S(2)}, u32[]{:S(2)}) collective-permute-start(f32[3,430,128]{2,1,0:T(8,128)S(1)} %get-tuple-element.33), channel_id=1, source_target_pairs={{1,0},{2,1},{3,2},{4,3},{5,4},{6,5},{7,6},{9,8},{10,9},{11,10},{12... | collective-permute-start | bytes 1981448 | tf_op jit(solution)/shard_map/ppermute | solution.py:31
  36.1 5.3 %collective-permute-done.2.left = f32[3,430,128]{2,1,0:T(8,128)S(1)} collective-permute-done((f32[3,430,128]{2,1,0:T(8,128)S(1)}, f32[3,430,128]{2,1,0:T(8,128)S(1)}, u32[]{:S(2)}, u32[]{:S(2)}) %collective-permute-start.2) | collective-permute-done | bytes 660512 | tf_op jit(solution)/shard_map/ppermute | solution.py:31
  41.4 4.5 %collective-permute-done.3.right = f32[3,430,128]{2,1,0:T(8,128)S(1)} collective-permute-done((f32[3,430,128]{2,1,0:T(8,128)S(1)}, f32[3,430,128]{2,1,0:T(8,128)S(1)}, u32[]{:S(2)}, u32[]{:S(2)}) %collective-permute-start.3) | collective-permute-done | bytes 660512 | tf_op jit(solution)/shard_map/ppermute | solution.py:31
  45.9 8.3 %core0.1 = (f32[4,12,32,128]{3,2,1,0:T(8,128)S(1)}, f32[1,8,128]{2,1,0:T(8,128)S(1)}) custom-call(f32[8,128]{1,0:T(8,128)S(1)} %early.1.before_ref, bf16[32,12,32,128]{3,2,1,0:T(8,128)(2,1)S(1)} %copy-done.1, f32[3,12,32,128]{3,2,1,0:T(8,128)S(1)} %copy-done.8, f32[3,480,128]{2,1,0:T(8,128)S(1)} %collective-permute-done.lo_ref.lo, ...), custom_call_target="tpu_custom_call" | custom-call | flops 20000000000 | bytes 40000000 | tf_op jit(solution)/shard_map/core0/pallas_call | solution.py:435
  54.3 8.6 %core1.1 = (f32[4,12,32,128]{3,2,1,0:T(8,128)S(1)}, f32[1,8,128]{2,1,0:T(8,128)S(1)}) custom-call(f32[8,128]{1,0:T(8,128)S(1)} %bitcast.6, bf16[32,12,32,128]{3,2,1,0:T(8,128)(2,1)S(1)} %copy-done.1, f32[3,12,32,128]{3,2,1,0:T(8,128)S(1)} %copy-done.8, f32[3,480,128]{2,1,0:T(8,128)S(1)} %collective-permute-done.lo_ref.lo, ...), custom_call_target="tpu_custom_call" | custom-call | flops 20000000000 | bytes 40000000 | tf_op jit(solution)/shard_map/core1/pallas_call | solution.py:435
  62.9 8.4 %core2.1 = (f32[4,12,32,128]{3,2,1,0:T(8,128)S(1)}, f32[8,8,128]{2,1,0:T(8,128)S(1)}) custom-call(f32[8,128]{1,0:T(8,128)S(1)} %bitcast.5, bf16[32,12,32,128]{3,2,1,0:T(8,128)(2,1)S(1)} %copy-done.1, f32[3,12,32,128]{3,2,1,0:T(8,128)S(1)} %copy-done.8, f32[3,480,128]{2,1,0:T(8,128)S(1)} %collective-permute-done.lo_ref.lo, ...), custom_call_target="tpu_custom_call" | custom-call | flops 20000000000 | bytes 40000000 | tf_op jit(solution)/shard_map/core2/pallas_call | solution.py:435
  71.3 0.9 copy-done.3
  72.2 8.6 %all_to_all.10 = f32[8,8,128]{2,1,0:T(8,128)S(1)} all-to-all(f32[8,8,128]{2,1,0:T(8,128)S(1)} %get-tuple-element.36), channel_id=1, replica_groups=mesh['depth'=32,'height'=8] {'height'}, dimensions={0} | all-to-all | bytes 65536 | tf_op jit(solution)/shard_map/all_to_all | solution.py:572
  80.9 22.1 %all_to_all.11.s_ref = f32[32,8,128]{2,1,0:T(8,128)S(1)} all-to-all(f32[32,8,128]{2,1,0:T(8,128)S(1)} %broadcast_in_dim.2), channel_id=1, replica_groups=mesh['depth'=32,'height'=8] {'depth'}, dimensions={0} | all-to-all | bytes 262144 | tf_op jit(solution)/shard_map/all_to_all | solution.py:574
  103.0 1.1 %copy-done.4 = f32[4,12,32,128]{3,2,1,0:T(8,128)S(1)} copy-done((f32[4,12,32,128]{3,2,1,0:T(8,128)S(1)}, f32[4,12,32,128]{3,2,1,0:T(8,128)}, u32[]{:S(2)}) %copy-start.4) | copy-done | bytes 786456
  104.1 3.6 %tail.1 = (bf16[32,12,32,128]{3,2,1,0:T(8,128)(2,1)}, f32[1,1]{1,0:T(1,128)}, f32[3,32]{1,0:T(4,128)}, f32[1,3]{1,0:T(1,128)}) custom-call(f32[3,32,128]{2,1,0:T(8,128)S(1)} %copy-done.9, f32[32,8,128]{2,1,0:T(8,128)S(1)} %all_to_all.11.s_ref, f32[4,12,32,128]{3,2,1,0:T(8,128)S(1)} %get-tuple-element.37.refs_0_, ...), custom_call_target="tpu_custom_call" | custom-call | tf_op jit(solution)/shard_map/tail/pallas_call | solution.py:533
  (15 shorter events, 0.0 us)
Async XLA Ops:
  0.6 10.3 %copy-start.2 = (s32[3,12,32,128]{3,2,1,0:T(8,128)S(1)}, s32[3,12,32,128]{3,2,1,0:T(8,128)}, u32[]{:S(2)}) copy-start(s32[3,12,32,128]{3,2,1,0:T(8,128)} %l_own.5) | copy-start | bytes 1769476
  0.6 10.3 %copy-start.5 = (s32[3,12,32,128]{3,2,1,0:T(8,128)S(1)}, s32[3,12,32,128]{3,2,1,0:T(8,128)}, u32[]{:S(2)}) copy-start(s32[3,12,32,128]{3,2,1,0:T(8,128)} %k_own.5) | copy-start | bytes 1769476
  5.5 19.5 %collective-permute-start = (f32[3,480,128]{2,1,0:T(8,128)}, f32[3,480,128]{2,1,0:T(8,128)S(1)}, u32[]{:S(2)}, u32[]{:S(2)}) collective-permute-start(f32[3,480,128]{2,1,0:T(8,128)} %get-tuple-element.25), channel_id=1, source_target_pairs={{0,8},{8,16},{16,24},{24,32},{32,40},{40,48},{48,56},{56,64},{64,7... | collective-permute-start | bytes 2211848 | tf_op jit(solution)/shard_map/ppermute | solution.py:31
  9.6 19.1 %collective-permute-start.1 = (f32[3,480,128]{2,1,0:T(8,128)}, f32[3,480,128]{2,1,0:T(8,128)S(1)}, u32[]{:S(2)}, u32[]{:S(2)}) collective-permute-start(f32[3,480,128]{2,1,0:T(8,128)} %get-tuple-element.26), channel_id=1, source_target_pairs={{8,0},{16,8},{24,16},{32,24},{40,32},{48,40},{56,48},{64,56},{72,6... | collective-permute-start | bytes 2211848 | tf_op jit(solution)/shard_map/ppermute | solution.py:31
  11.0 1.9 %copy-start = (bf16[32,12,32,128]{3,2,1,0:T(8,128)(2,1)S(1)}, bf16[32,12,32,128]{3,2,1,0:T(8,128)(2,1)}, u32[]{:S(2)}) copy-start(bf16[32,12,32,128]{3,2,1,0:T(8,128)(2,1)} %f_ref.7) | copy-start | bytes 9437188
  12.8 1.1 copy-start.6
  13.9 14.9 %copy-start.8 = (f32[3,12,32,128]{3,2,1,0:T(8,128)S(1)}, f32[3,12,32,128]{3,2,1,0:T(8,128)}, u32[]{:S(2)}) copy-start(f32[3,12,32,128]{3,2,1,0:T(8,128)} %get-tuple-element.29.own_ref.e_own) | copy-start | bytes 1769476
  13.9 32.0 %copy-start.1 = (bf16[32,12,32,128]{3,2,1,0:T(8,128)(2,1)S(1)}, bf16[32,12,32,128]{3,2,1,0:T(8,128)(2,1)}, u32[]{:S(2)}) copy-start(bf16[32,12,32,128]{3,2,1,0:T(8,128)(2,1)} %f_ref.7) | copy-start | bytes 9437188
  28.9 12.5 %collective-permute-start.2 = (f32[3,430,128]{2,1,0:T(8,128)S(1)}, f32[3,430,128]{2,1,0:T(8,128)S(1)}, u32[]{:S(2)}, u32[]{:S(2)}) collective-permute-start(f32[3,430,128]{2,1,0:T(8,128)S(1)} %get-tuple-element.32), channel_id=1, source_target_pairs={{0,1},{1,2},{2,3},{3,4},{4,5},{5,6},{6,7},{8,9},{9,10},{10,11},{11... | collective-permute-start | bytes 1981448 | tf_op jit(solution)/shard_map/ppermute | solution.py:31
  33.8 20.5 %copy-start.7 = (f32[3,12,32,128]{3,2,1,0:T(8,128)S(1)}, f32[3,12,32,128]{3,2,1,0:T(8,128)}, u32[]{:S(2)}) copy-start(f32[3,12,32,128]{3,2,1,0:T(8,128)} %get-tuple-element.27.p_ref.p_own) | copy-start | bytes 1769476
  33.8 12.1 %collective-permute-start.3 = (f32[3,430,128]{2,1,0:T(8,128)S(1)}, f32[3,430,128]{2,1,0:T(8,128)S(1)}, u32[]{:S(2)}, u32[]{:S(2)}) collective-permute-start(f32[3,430,128]{2,1,0:T(8,128)S(1)} %get-tuple-element.33), channel_id=1, source_target_pairs={{1,0},{2,1},{3,2},{4,3},{5,4},{6,5},{7,6},{9,8},{10,9},{11,10},{12... | collective-permute-start | bytes 1981448 | tf_op jit(solution)/shard_map/ppermute | solution.py:31
  62.9 40.1 %copy-start.9 = (f32[3,32,128]{2,1,0:T(8,128)S(1)}, f32[3,32,128]{2,1,0:T(8,128)}, u32[]{:S(2)}) copy-start(f32[3,32,128]{2,1,0:T(8,128)} %get-tuple-element.24.w_ref) | copy-start | bytes 147460
  71.3 0.9 copy-start.3
  103.0 1.1 %copy-start.4 = (f32[4,12,32,128]{3,2,1,0:T(8,128)S(1)}, f32[4,12,32,128]{3,2,1,0:T(8,128)}, u32[]{:S(2)}) copy-start(f32[4,12,32,128]{3,2,1,0:T(8,128)} %copy-done.3) | copy-start | bytes 2359300

commit v3 on v2

--- a/solution.py
+++ b/solution.py
@@ -453,6 +453,23 @@
     )(*args)
 
 
+def middle_kernel(in_ref, out_ref):
+    total = jnp.sum(in_ref[...], axis=0)
+    for n in range(out_ref.shape[0]):
+        out_ref[n] = total
+
+
+def run_middle(copies, parts):
+    return pl.pallas_call(
+        middle_kernel,
+        in_specs=[VMEM],
+        out_specs=VMEM,
+        out_shape=jax.ShapeDtypeStruct((copies,) + parts.shape[1:], jnp.float32),
+        compiler_params=pltpu.CompilerParams(vmem_limit_bytes=2 * 2**20),
+        name="middle",
+    )(parts)
+
+
 def tail_kernel(cells, w_ref, s_ref, *refs):
     classes = len(refs) - 5
     x_ref = refs[:classes]
@@ -569,8 +586,7 @@
         fields.append(mine)
         if copies == 1:
             local = local[0]
-    part = jnp.sum(lax.all_to_all(local, "height", 0, 0, tiled=True), axis=0)
-    part = jnp.broadcast_to(part[None], (lax.axis_size("depth"),) + part.shape)
+    part = run_middle(lax.axis_size("depth"), lax.all_to_all(local, "height", 0, 0, tiled=True))
     parts = lax.all_to_all(part, "depth", 0, 0, tiled=True)
     grad_features, loss, grad_w, grad_b = run_tail(cells, spread, parts, fields)
     return loss[0, 0], grad_features, grad_w, grad_b[0]

time: 108 us -> 106 us (0.981)
  local copies, waits for them, and re-layouts: 5.03 us -> 2.97 us
    unnamed x20 -> x16, local copies, waits for them, and re-layouts: 5.01 us -> 2.97 us
where the time goes in v3:
time: 106 us
  Pallas kernels  36.9 us (35%)
  blocking collectives  30.7 us (29%)
  waiting for transfers between devices  21.8 us (21%)
  starting transfers between devices  12.3 us (12%)
  local copies, waits for them, and re-layouts  2.97 us (3%)
    pallas_call x3, Pallas kernels, run_core(): pl.pallas_call(functools.partial(core_kernel, k, classes), in_specs=[VMEM...  25.3 us
    all_to_all x1, blocking collectives, per_device(): parts = lax.all_to_all(part, 'depth', 0, 0, tiled=True)  22.1 us
    ppermute x4, waiting for transfers between devices, shift(): return lax.ppermute(value, axis, pairs)  21.8 us
    ppermute x4, starting transfers between devices, shift(): return lax.ppermute(value, axis, pairs)  12.3 us
    all_to_all x1, blocking collectives, per_device(): lax.all_to_all(local, 'height', 0, 0, tiled=True)  8.65 us
    pallas_call x1, Pallas kernels, run_head(): pl.pallas_call(head_kernel, in_specs=[HBM] * 4, out_specs=[VMEM] * 5, out...  4.89 us
    pallas_call x1, Pallas kernels, run_tail(): pl.pallas_call(functools.partial(tail_kernel, cells), grid=(depth // step...  3.65 us
    unnamed x16, local copies, waits for them, and re-layouts  2.97 us
  transfers between devices with their start and end apart: 4, of which 4 were waited for; matrix products, arithmetic and copies ran while one was open for 0% of the time, Pallas kernels for 3%

profile of v3, /device:TPU:1, one launch (start us, length us, event | category | flops | bytes accessed | tf_op | source)
XLA Modules:
  0.0 105.5 jit_solution(14207690324398956770)
XLA Ops:
  0.6 0.0 copy-start.2
  0.6 0.0 copy-start.3
  0.7 4.9 %head.1 = (f32[3,12,32,128]{3,2,1,0:T(8,128)}, f32[3,12,32,128]{3,2,1,0:T(8,128)}, f32[3,480,128]{2,1,0:T(8,128)}, f32[3,480,128]{2,1,0:T(8,128)}, f32[3,32,128]{2,1,0:T(8,128)}) custom-call(bf16[3,32]{1,0:T(4,128)(2,1)} %w_hbm.1, f32[1,3]{1,0:T(1,128)} %bitcast.7, bf16[32,12,32,128]{3,2,1,0:T(8,128)(2,1)} %f_ref.7, s32[3,12,32,128]{3,2,1,0:T(8,128)} %l_own.5), custom_call_target="tpu_custom_call" | custom-call | tf_op jit(solution)/shard_map/head/pallas_call | solution.py:92
  5.5 4.1 %collective-permute-start = (f32[3,480,128]{2,1,0:T(8,128)}, f32[3,480,128]{2,1,0:T(8,128)S(1)}, u32[]{:S(2)}, u32[]{:S(2)}) collective-permute-start(f32[3,480,128]{2,1,0:T(8,128)} %get-tuple-element.25), channel_id=1, source_target_pairs={{0,8},{8,16},{16,24},{24,32},{32,40},{40,48},{48,56},{56,64},{64,7... | collective-permute-start | bytes 2211848 | tf_op jit(solution)/shard_map/ppermute | solution.py:31
  9.6 1.3 %collective-permute-start.1 = (f32[3,480,128]{2,1,0:T(8,128)}, f32[3,480,128]{2,1,0:T(8,128)S(1)}, u32[]{:S(2)}, u32[]{:S(2)}) collective-permute-start(f32[3,480,128]{2,1,0:T(8,128)} %get-tuple-element.26), channel_id=1, source_target_pairs={{8,0},{16,8},{24,16},{32,24},{40,32},{48,40},{56,48},{64,56},{72,6... | collective-permute-start | bytes 2211848 | tf_op jit(solution)/shard_map/ppermute | solution.py:31
  10.9 0.0 copy-done.2
  11.0 0.0 copy-start
  11.0 1.9 %copy-done = bf16[32,12,32,128]{3,2,1,0:T(8,128)(2,1)S(1)} copy-done((bf16[32,12,32,128]{3,2,1,0:T(8,128)(2,1)S(1)}, bf16[32,12,32,128]{3,2,1,0:T(8,128)(2,1)}, u32[]{:S(2)}) %copy-start) | copy-done | bytes 3145752
  12.8 1.1 %copy-done.4 = f32[3,12,32,128]{3,2,1,0:T(8,128)S(1)} copy-done((f32[3,12,32,128]{3,2,1,0:T(8,128)S(1)}, f32[3,12,32,128]{3,2,1,0:T(8,128)}, u32[]{:S(2)}) %copy-start.4) | copy-done | bytes 589848
  13.9 2.9 %early.1.before_ref = f32[8,128]{1,0:T(8,128)S(1)} custom-call(bf16[32,12,32,128]{3,2,1,0:T(8,128)(2,1)S(1)} %copy-done, s32[3,12,32,128]{3,2,1,0:T(8,128)S(1)} %copy-done.2, f32[3,12,32,128]{3,2,1,0:T(8,128)S(1)} %copy-done.4, s32[3,12,32,128]{3,2,1,0:T(8,128)S(1)} %copy-done.3), custom_call_target="tpu_custom_call" | custom-call | flops 1000000000 | bytes 10000000 | tf_op jit(solution)/shard_map/early/pallas_call | solution.py:216
  16.8 8.2 %collective-permute-done.lo_ref.lo = f32[3,480,128]{2,1,0:T(8,128)S(1)} collective-permute-done((f32[3,480,128]{2,1,0:T(8,128)}, f32[3,480,128]{2,1,0:T(8,128)S(1)}, u32[]{:S(2)}, u32[]{:S(2)}) %collective-permute-start) | collective-permute-done | bytes 737312 | tf_op jit(solution)/shard_map/ppermute | solution.py:31
  25.0 3.7 %collective-permute-done.1.hi_ref.hi = f32[3,480,128]{2,1,0:T(8,128)S(1)} collective-permute-done((f32[3,480,128]{2,1,0:T(8,128)}, f32[3,480,128]{2,1,0:T(8,128)S(1)}, u32[]{:S(2)}, u32[]{:S(2)}) %collective-permute-start.1) | collective-permute-done | bytes 737312 | tf_op jit(solution)/shard_map/ppermute | solution.py:31
  28.8 0.2 side.1
  28.9 4.9 %collective-permute-start.2 = (f32[3,430,128]{2,1,0:T(8,128)S(1)}, f32[3,430,128]{2,1,0:T(8,128)S(1)}, u32[]{:S(2)}, u32[]{:S(2)}) collective-permute-start(f32[3,430,128]{2,1,0:T(8,128)S(1)} %get-tuple-element.32), channel_id=1, source_target_pairs={{0,1},{1,2},{2,3},{3,4},{4,5},{5,6},{6,7},{8,9},{9,10},{10,11},{11... | collective-permute-start | bytes 1981448 | tf_op jit(solution)/shard_map/ppermute | solution.py:31
  33.8 2.1 %collective-permute-start.3 = (f32[3,430,128]{2,1,0:T(8,128)S(1)}, f32[3,430,128]{2,1,0:T(8,128)S(1)}, u32[]{:S(2)}, u32[]{:S(2)}) collective-permute-start(f32[3,430,128]{2,1,0:T(8,128)S(1)} %get-tuple-element.33), channel_id=1, source_target_pairs={{1,0},{2,1},{3,2},{4,3},{5,4},{6,5},{7,6},{9,8},{10,9},{11,10},{12... | collective-permute-start | bytes 1981448 | tf_op jit(solution)/shard_map/ppermute | solution.py:31
  35.9 5.5 %collective-permute-done.2.left = f32[3,430,128]{2,1,0:T(8,128)S(1)} collective-permute-done((f32[3,430,128]{2,1,0:T(8,128)S(1)}, f32[3,430,128]{2,1,0:T(8,128)S(1)}, u32[]{:S(2)}, u32[]{:S(2)}) %collective-permute-start.2) | collective-permute-done | bytes 660512 | tf_op jit(solution)/shard_map/ppermute | solution.py:31
  41.4 4.4 %collective-permute-done.3.right = f32[3,430,128]{2,1,0:T(8,128)S(1)} collective-permute-done((f32[3,430,128]{2,1,0:T(8,128)S(1)}, f32[3,430,128]{2,1,0:T(8,128)S(1)}, u32[]{:S(2)}, u32[]{:S(2)}) %collective-permute-start.3) | collective-permute-done | bytes 660512 | tf_op jit(solution)/shard_map/ppermute | solution.py:31
  45.8 0.0 copy-done.1
  45.8 8.3 %core0.1 = (f32[4,12,32,128]{3,2,1,0:T(8,128)S(1)}, f32[1,8,128]{2,1,0:T(8,128)S(1)}) custom-call(f32[8,128]{1,0:T(8,128)S(1)} %early.1.before_ref, bf16[32,12,32,128]{3,2,1,0:T(8,128)(2,1)S(1)} %copy-done.1, f32[3,12,32,128]{3,2,1,0:T(8,128)S(1)} %copy-done.6, f32[3,480,128]{2,1,0:T(8,128)S(1)} %collective-permute-done.lo_ref.lo, ...), custom_call_target="tpu_custom_call" | custom-call | flops 20000000000 | bytes 40000000 | tf_op jit(solution)/shard_map/core0/pallas_call | solution.py:435
  54.1 8.6 %core1.1 = (f32[4,12,32,128]{3,2,1,0:T(8,128)S(1)}, f32[1,8,128]{2,1,0:T(8,128)S(1)}) custom-call(f32[8,128]{1,0:T(8,128)S(1)} %bitcast.6, bf16[32,12,32,128]{3,2,1,0:T(8,128)(2,1)S(1)} %copy-done.1, f32[3,12,32,128]{3,2,1,0:T(8,128)S(1)} %copy-done.6, f32[3,480,128]{2,1,0:T(8,128)S(1)} %collective-permute-done.lo_ref.lo, ...), custom_call_target="tpu_custom_call" | custom-call | flops 20000000000 | bytes 40000000 | tf_op jit(solution)/shard_map/core1/pallas_call | solution.py:435
  62.7 8.4 %core2.1 = (f32[4,12,32,128]{3,2,1,0:T(8,128)S(1)}, f32[8,8,128]{2,1,0:T(8,128)S(1)}) custom-call(f32[8,128]{1,0:T(8,128)S(1)} %bitcast.5, bf16[32,12,32,128]{3,2,1,0:T(8,128)(2,1)S(1)} %copy-done.1, f32[3,12,32,128]{3,2,1,0:T(8,128)S(1)} %copy-done.6, f32[3,480,128]{2,1,0:T(8,128)S(1)} %collective-permute-done.lo_ref.lo, ...), custom_call_target="tpu_custom_call" | custom-call | flops 20000000000 | bytes 40000000 | tf_op jit(solution)/shard_map/core2/pallas_call | solution.py:435
  71.1 8.6 %all_to_all.10.in_ref = f32[8,8,128]{2,1,0:T(8,128)S(1)} all-to-all(f32[8,8,128]{2,1,0:T(8,128)S(1)} %get-tuple-element.36), channel_id=1, replica_groups=mesh['depth'=32,'height'=8] {'height'}, dimensions={0} | all-to-all | bytes 65536 | tf_op jit(solution)/shard_map/all_to_all | solution.py:589
  79.8 22.1 %all_to_all.11.s_ref = f32[32,8,128]{2,1,0:T(8,128)S(1)} all-to-all(f32[32,8,128]{2,1,0:T(8,128)S(1)} %middle.1), channel_id=1, replica_groups=mesh['depth'=32,'height'=8] {'depth'}, dimensions={0} | all-to-all | bytes 262144 | tf_op jit(solution)/shard_map/all_to_all | solution.py:590
  101.9 3.6 %tail.1 = (bf16[32,12,32,128]{3,2,1,0:T(8,128)(2,1)}, f32[1,1]{1,0:T(1,128)}, f32[3,32]{1,0:T(4,128)}, f32[1,3]{1,0:T(1,128)}) custom-call(f32[3,32,128]{2,1,0:T(8,128)S(1)} %copy-done.7, f32[32,8,128]{2,1,0:T(8,128)S(1)} %all_to_all.11.s_ref, f32[4,12,32,128]{3,2,1,0:T(8,128)S(1)} %get-tuple-element.37.refs_0_, ...), custom_call_target="tpu_custom_call" | custom-call | tf_op jit(solution)/shard_map/tail/pallas_call | solution.py:550
  (10 shorter events, 0.0 us)
Async XLA Ops:
  0.6 10.3 %copy-start.2 = (s32[3,12,32,128]{3,2,1,0:T(8,128)S(1)}, s32[3,12,32,128]{3,2,1,0:T(8,128)}, u32[]{:S(2)}) copy-start(s32[3,12,32,128]{3,2,1,0:T(8,128)} %l_own.5) | copy-start | bytes 1769476
  0.6 10.3 %copy-start.3 = (s32[3,12,32,128]{3,2,1,0:T(8,128)S(1)}, s32[3,12,32,128]{3,2,1,0:T(8,128)}, u32[]{:S(2)}) copy-start(s32[3,12,32,128]{3,2,1,0:T(8,128)} %k_own.5) | copy-start | bytes 1769476
  5.5 19.5 %collective-permute-start = (f32[3,480,128]{2,1,0:T(8,128)}, f32[3,480,128]{2,1,0:T(8,128)S(1)}, u32[]{:S(2)}, u32[]{:S(2)}) collective-permute-start(f32[3,480,128]{2,1,0:T(8,128)} %get-tuple-element.25), channel_id=1, source_target_pairs={{0,8},{8,16},{16,24},{24,32},{32,40},{40,48},{48,56},{56,64},{64,7... | collective-permute-start | bytes 2211848 | tf_op jit(solution)/shard_map/ppermute | solution.py:31
  9.6 19.1 %collective-permute-start.1 = (f32[3,480,128]{2,1,0:T(8,128)}, f32[3,480,128]{2,1,0:T(8,128)S(1)}, u32[]{:S(2)}, u32[]{:S(2)}) collective-permute-start(f32[3,480,128]{2,1,0:T(8,128)} %get-tuple-element.26), channel_id=1, source_target_pairs={{8,0},{16,8},{24,16},{32,24},{40,32},{48,40},{56,48},{64,56},{72,6... | collective-permute-start | bytes 2211848 | tf_op jit(solution)/shard_map/ppermute | solution.py:31
  11.0 1.9 %copy-start = (bf16[32,12,32,128]{3,2,1,0:T(8,128)(2,1)S(1)}, bf16[32,12,32,128]{3,2,1,0:T(8,128)(2,1)}, u32[]{:S(2)}) copy-start(bf16[32,12,32,128]{3,2,1,0:T(8,128)(2,1)} %f_ref.7) | copy-start | bytes 9437188
  12.8 1.1 %copy-start.4 = (f32[3,12,32,128]{3,2,1,0:T(8,128)S(1)}, f32[3,12,32,128]{3,2,1,0:T(8,128)}, u32[]{:S(2)}) copy-start(f32[3,12,32,128]{3,2,1,0:T(8,128)} %get-tuple-element.27.p_ref.p_own) | copy-start | bytes 1769476
  13.9 14.9 %copy-start.6 = (f32[3,12,32,128]{3,2,1,0:T(8,128)S(1)}, f32[3,12,32,128]{3,2,1,0:T(8,128)}, u32[]{:S(2)}) copy-start(f32[3,12,32,128]{3,2,1,0:T(8,128)} %get-tuple-element.29.own_ref.e_own) | copy-start | bytes 1769476
  13.9 31.9 %copy-start.1 = (bf16[32,12,32,128]{3,2,1,0:T(8,128)(2,1)S(1)}, bf16[32,12,32,128]{3,2,1,0:T(8,128)(2,1)}, u32[]{:S(2)}) copy-start(bf16[32,12,32,128]{3,2,1,0:T(8,128)(2,1)} %f_ref.7) | copy-start | bytes 9437188
  13.9 31.9 %copy-start.5 = (f32[3,12,32,128]{3,2,1,0:T(8,128)S(1)}, f32[3,12,32,128]{3,2,1,0:T(8,128)}, u32[]{:S(2)}) copy-start(f32[3,12,32,128]{3,2,1,0:T(8,128)} %get-tuple-element.27.p_ref.p_own) | copy-start | bytes 1769476
  28.9 12.5 %collective-permute-start.2 = (f32[3,430,128]{2,1,0:T(8,128)S(1)}, f32[3,430,128]{2,1,0:T(8,128)S(1)}, u32[]{:S(2)}, u32[]{:S(2)}) collective-permute-start(f32[3,430,128]{2,1,0:T(8,128)S(1)} %get-tuple-element.32), channel_id=1, source_target_pairs={{0,1},{1,2},{2,3},{3,4},{4,5},{5,6},{6,7},{8,9},{9,10},{10,11},{11... | collective-permute-start | bytes 1981448 | tf_op jit(solution)/shard_map/ppermute | solution.py:31
  33.8 12.0 %collective-permute-start.3 = (f32[3,430,128]{2,1,0:T(8,128)S(1)}, f32[3,430,128]{2,1,0:T(8,128)S(1)}, u32[]{:S(2)}, u32[]{:S(2)}) collective-permute-start(f32[3,430,128]{2,1,0:T(8,128)S(1)} %get-tuple-element.33), channel_id=1, source_target_pairs={{1,0},{2,1},{3,2},{4,3},{5,4},{6,5},{7,6},{9,8},{10,9},{11,10},{12... | collective-permute-start | bytes 1981448 | tf_op jit(solution)/shard_map/ppermute | solution.py:31
  62.7 39.2 %copy-start.7 = (f32[3,32,128]{2,1,0:T(8,128)S(1)}, f32[3,32,128]{2,1,0:T(8,128)}, u32[]{:S(2)}) copy-start(f32[3,32,128]{2,1,0:T(8,128)} %get-tuple-element.24.w_ref) | copy-start | bytes 147460
